TPU v7x, 128 devices: a whole 4x4x4 slice. The times are simulated.
128 devices in a mesh: ep: 16 (over x, z_hi, core), tp: 8 (over y, z_lo).
Axes of the slice: x: 4, y: 4, z: 4 (z_hi: 2, z_lo: 2; z = z_hi * 2 + z_lo), core: 2. Of those that a mesh axis runs over, the one named last changes fastest.
Arguments:
- tokens: bfloat16 [2048, 7168], P(('ep', 'tp')), may hold values from -6 to 6
- cotangent: bfloat16 [2048, 7168], P(('ep', 'tp')), may hold values from -6 to 6
- route_ids: int32 [2048, 2], P('ep'), may hold values from 0 to 63, all different within a row; in each aligned block of 128 rows (0 to 127, 128 to 255, ...) at most 6 rows name the same one
- route_probs: float32 [2048, 2], P('ep'), may hold values from 0.2 to 1
- dense_gate: bfloat16 [7168, 2432], P('ep', 'tp'), may hold values from -0.0625 to 0.0625
- dense_up: bfloat16 [7168, 2432], P('ep', 'tp'), may hold values from -0.0625 to 0.0625
- dense_down: bfloat16 [2432, 7168], P('tp', 'ep'), may hold values from -0.125 to 0.125
- expert_gate: bfloat16 [128, 192, 7168], P(('ep', 'tp')), may hold values from -0.0625 to 0.0625
- expert_up: bfloat16 [128, 192, 7168], P(('ep', 'tp')), may hold values from -0.0625 to 0.0625
- expert_down: bfloat16 [128, 192, 7168], P(('ep', 'tp')), may hold values from -0.3125 to 0.3125
Outputs:
- grad_tokens: bfloat16 [2048, 7168], P(('ep', 'tp'))
- grad_dense_gate: bfloat16 [7168, 2432], P('ep', 'tp')
- grad_dense_up: bfloat16 [7168, 2432], P('ep', 'tp')
- grad_dense_down: bfloat16 [2432, 7168], P('tp', 'ep')
- grad_expert_gate: bfloat16 [128, 192, 7168], P(('ep', 'tp'))
- grad_expert_up: bfloat16 [128, 192, 7168], P(('ep', 'tp'))
- grad_expert_down: bfloat16 [128, 192, 7168], P(('ep', 'tp'))
Inputs may be any that keep to these rules, and one draw needn't show every extreme that they name: `route_ids`: each token names two different experts; within each aligned block of 128 tokens no expert is named more than 6 times, and in some block an expert is named exactly 6 times; every expert is named by some token.
All inputs are finite; a program needn't handle non-finite values.
Results may differ from a plain program's by a relative error of at most 0.024.
Values may be sent and summed in bfloat16 or wider, within the bound.
A program may use at most 128 MiB of HBM per device.

v0:
```python
import math

import jax
import jax.numpy as jnp
from jax import lax
from jax.sharding import PartitionSpec as P


def product(left, right):
    return jnp.dot(left, right, preferred_element_type=jnp.float32)


def product_t(left, right):
    return lax.dot_general(
        left, right, (((1,), (1,)), ((), ())), preferred_element_type=jnp.float32
    )


def product_left(left, right):
    return lax.dot_general(
        left, right, (((0,), (0,)), ((), ())), preferred_element_type=jnp.float32
    )


def unit_grads(gate_pre, up_pre, d_hidden):
    sigmoid_gate = jax.nn.sigmoid(gate_pre)
    activated = gate_pre * sigmoid_gate
    hidden = (activated * up_pre).astype(jnp.bfloat16)
    d_gate = (d_hidden * up_pre * sigmoid_gate * (1.0 + gate_pre * (1.0 - sigmoid_gate))).astype(
        jnp.bfloat16
    )
    d_up = (d_hidden * activated).astype(jnp.bfloat16)
    return (hidden, d_gate, d_up)


def rounded_term(value):
    return lax.optimization_barrier(value.astype(jnp.bfloat16)).astype(jnp.float32)


def per_device(
    tokens,
    cotangent,
    route_ids,
    route_probs,
    dense_gate,
    dense_up,
    dense_down,
    expert_gate,
    expert_up,
    expert_down,
):
    ep_count = lax.axis_size("ep")
    tp_count = lax.axis_size("tp")
    tok_rows, width = tokens.shape
    group = tok_rows * tp_count
    total_tokens = group * ep_count
    experts_all = ep_count * tp_count // 2
    capacity = max(2, 3 * group // experts_all)
    scale_dense = 1.0 / math.sqrt(total_tokens)
    scale_expert = math.sqrt(experts_all / (2.0 * total_tokens))
    grp_tokens, grp_cot = (
        lax.all_gather(tokens, "tp", axis=0, tiled=True),
        lax.all_gather(cotangent, "tp", axis=0, tiled=True),
    )
    full_gate = lax.all_gather(dense_gate, "ep", axis=0, tiled=True)
    full_up = lax.all_gather(dense_up, "ep", axis=0, tiled=True)
    full_down = lax.all_gather(dense_down, "ep", axis=1, tiled=True)
    pre_gate = product(grp_tokens, full_gate)
    pre_up = product(grp_tokens, full_up)
    dense_dh = product_t(grp_cot, full_down)
    hidden, d_gate, d_up = unit_grads(pre_gate, pre_up, dense_dh)
    dense_dx = product_t(d_gate, full_gate) + product_t(d_up, full_up)
    columns = grp_tokens
    gate_sum = lax.psum_scatter(
        rounded_term(product_left(columns, d_gate)).astype(jnp.bfloat16),
        "ep",
        scatter_dimension=0,
        tiled=True,
    ).astype(jnp.float32)
    columns = grp_tokens
    up_sum = lax.psum_scatter(
        rounded_term(product_left(columns, d_up)).astype(jnp.bfloat16),
        "ep",
        scatter_dimension=0,
        tiled=True,
    ).astype(jnp.float32)
    columns = grp_cot
    down_sum = lax.psum_scatter(
        rounded_term(product_left(columns, hidden)).astype(jnp.bfloat16),
        "ep",
        scatter_dimension=0,
        tiled=True,
    ).astype(jnp.float32)
    grad_gate = (gate_sum * scale_dense).astype(jnp.bfloat16)
    grad_up = (up_sum * scale_dense).astype(jnp.bfloat16)
    grad_down = (down_sum * scale_dense).astype(jnp.bfloat16).T
    dense_dx, grad_dense_gate, grad_dense_up, grad_dense_down = (
        dense_dx,
        grad_gate,
        grad_up,
        grad_down,
    )
    tp_place = lax.axis_index("tp")
    targets = jnp.arange(ep_count, dtype=jnp.int32) * (tp_count // 2) + tp_place // 2
    flat_ids = route_ids.reshape(-1)
    match = (flat_ids[:, None] == targets[None, :]).astype(jnp.int32)
    rank = jnp.cumsum(match, axis=0, dtype=jnp.int32) - 1
    slots = jnp.arange(capacity, dtype=jnp.int32)
    pick = ((rank.T[:, None, :] == slots[None, :, None]) & (match.T[:, None, :] == 1)).astype(
        jnp.float32
    )
    pick = pick.reshape(ep_count, capacity, group, 2)
    select = jnp.sum(pick, axis=3)
    slot_prob = jnp.sum(pick * route_probs.reshape(1, 1, group, 2), axis=(2, 3))
    select_half = select.astype(jnp.bfloat16)
    send_rows = jnp.einsum(
        "jcn,nd->jcd", select_half, grp_tokens, preferred_element_type=jnp.float32
    ).astype(jnp.bfloat16)
    cot_rows = jnp.einsum("jcn,nd->jcd", select_half, grp_cot, preferred_element_type=jnp.float32)
    send_grads = (cot_rows * slot_prob[:, :, None]).astype(jnp.bfloat16)
    recv_rows = lax.all_to_all(send_rows, "ep", split_axis=0, concat_axis=0, tiled=True)
    recv_grads = lax.all_to_all(send_grads, "ep", split_axis=0, concat_axis=0, tiled=True)
    select, recv_rows, recv_grads = (select, recv_rows, recv_grads)
    slot_rows = ep_count * capacity
    rows_in = recv_rows.reshape(slot_rows, width)
    rows_grad = recv_grads.reshape(slot_rows, width)
    slice_gate = expert_gate[0]
    slice_up = expert_up[0]
    slice_down = expert_down[0]
    expert_pre_gate = product_t(rows_in, slice_gate)
    expert_pre_up = product_t(rows_in, slice_up)
    expert_dh = product_t(rows_grad, slice_down)
    expert_hidden, expert_dgate, expert_dup = unit_grads(expert_pre_gate, expert_pre_up, expert_dh)
    grad_expert_gate = (product_left(expert_dgate, rows_in) * scale_expert).astype(jnp.bfloat16)[
        None
    ]
    grad_expert_up = (product_left(expert_dup, rows_in) * scale_expert).astype(jnp.bfloat16)[None]
    grad_expert_down = (product_left(expert_hidden, rows_grad) * scale_expert).astype(jnp.bfloat16)[
        None
    ]
    back_rows = product(expert_dgate, slice_gate) + product(expert_dup, slice_up)
    returned = lax.all_to_all(
        back_rows.reshape(ep_count, capacity, width).astype(jnp.bfloat16),
        "ep",
        split_axis=0,
        concat_axis=0,
        tiled=True,
    ).astype(jnp.float32)
    moe_part = jnp.einsum("jcn,jcd->nd", select, returned, precision=lax.Precision.HIGHEST)
    summed = lax.psum_scatter(
        (dense_dx + moe_part).astype(jnp.bfloat16), "tp", scatter_dimension=0, tiled=True
    ).astype(jnp.float32)
    grad_tokens = (cotangent.astype(jnp.float32) + summed).astype(jnp.bfloat16)
    return (
        grad_tokens,
        grad_dense_gate,
        grad_dense_up,
        grad_dense_down,
        grad_expert_gate,
        grad_expert_up,
        grad_expert_down,
    )


def solution(mesh):
    return jax.shard_map(
        per_device,
        mesh=mesh,
        in_specs=(
            P(("ep", "tp"), None),
            P(("ep", "tp"), None),
            P("ep", None),
            P("ep", None),
            P("ep", "tp"),
            P("ep", "tp"),
            P("tp", "ep"),
            P(("ep", "tp"), None, None),
            P(("ep", "tp"), None, None),
            P(("ep", "tp"), None, None),
        ),
        out_specs=(
            P(("ep", "tp"), None),
            P("ep", "tp"),
            P("ep", "tp"),
            P("tp", "ep"),
            P(("ep", "tp"), None, None),
            P(("ep", "tp"), None, None),
            P(("ep", "tp"), None, None),
        ),
        check_vma=False,
    )
```

profile of v0, /device:TPU:1, one launch (start us, length us, event | category | flops | bytes accessed | tf_op | source)
XLA Modules:
  0.0 696.1 jit_solution(13369201884629283699)
XLA Ops:
  14.2 43.6 %all-gather.9.cloned.1.call-done = bf16[128,7168]{1,0:T(8,128)(2,1)} async-done(((bf16[16,7168]{1,0:T(8,128)(2,1)}), bf16[128,7168]{1,0:T(8,128)(2,1)}) %all-gather.9.cloned.1.call-update) | async-done | bytes 1835024 | tf_op jit(solution)/shard_map/all_gather | solution.py:63
  61.9 10.1 %all-to-all-start = ((bf16[16,6,7168]{2,1,0:T(8,128)(2,1)}), bf16[16,6,7168]{2,1,0:T(8,128)(2,1)}, u32[]{:S(2)}, u32[]{:S(2)}) async-start(bf16[16,6,7168]{2,1,0:T(8,128)(2,1)} %copy.49), calls=%async_computation | async-start | bytes 3670016 | tf_op jit(solution)/shard_map/all_to_all | solution.py:122
  72.0 55.9 %all-gather.11.cloned.1.call-done = bf16[128,7168]{1,0:T(8,128)(2,1)} async-done(((bf16[16,7168]{1,0:T(8,128)(2,1)}), bf16[128,7168]{1,0:T(8,128)(2,1)}) %all-gather.11.cloned.1.call-update) | async-done | bytes 1835024 | tf_op jit(solution)/shard_map/all_gather | solution.py:62
  131.9 8.7 %all-to-all-start.1 = ((bf16[16,6,7168]{2,1,0:T(8,128)(2,1)}), bf16[16,6,7168]{2,1,0:T(8,128)(2,1)}, u32[]{:S(2)}, u32[]{:S(2)}) async-start(bf16[16,6,7168]{2,1,0:T(8,128)(2,1)} %copy.50), calls=%async_computation.1 | async-start | bytes 3670016 | tf_op jit(solution)/shard_map/all_to_all | solution.py:121
  143.4 27.4 %all-to-all-done.1 = bf16[16,6,7168]{2,1,0:T(8,128)(2,1)} async-done(((bf16[16,6,7168]{2,1,0:T(8,128)(2,1)}), bf16[16,6,7168]{2,1,0:T(8,128)(2,1)}, u32[]{:S(2)}, u32[]{:S(2)}) %all-to-all-start.1) | async-done | bytes 1376288 | tf_op jit(solution)/shard_map/all_to_all | solution.py:121
  183.6 34.4 %all_to_all.15 = bf16[16,6,7168]{2,1,0:T(8,128)(2,1)S(1)} all-to-all(bf16[16,6,7168]{2,1,0:T(8,128)(2,1)S(1)} %convert_element_type.125), channel_id=1, replica_groups=mesh['ep'=16,'tp'=8] {'ep'}, dimensions={0} | all-to-all | bytes 2752512 | tf_op jit(solution)/shard_map/all_to_all | solution.py:142
  218.0 4.0 convolution_bitcast_fusion
  221.9 7.4 %copy.45 = bf16[16,448,304]{1,0,2:T(8,128)(2,1)} copy(bf16[16,448,304]{1,2,0:T(8,128)(2,1)} %all-gather.17.cloned.1.call-done) | data formatting | bytes 8716288 | tf_op jit(solution)/shard_map/all_gather | solution.py:65
  229.4 9.0 %reshape.100 = bf16[7168,304]{0,1:T(8,128)(2,1)} reshape(bf16[16,448,304]{1,0,2:T(8,128)(2,1)} %copy.45) | data formatting | bytes 8716288
  238.4 45.2 %all-gather.15.cloned.1.call-done = bf16[16,448,304]{1,2,0:T(8,128)(2,1)} async-done(((bf16[1,448,304]{1,2,0:T(8,128)(2,1)}), bf16[16,448,304]{1,2,0:T(8,128)(2,1)}) %all-gather.15.cloned.1.call-update) | async-done | bytes 4358160 | tf_op jit(solution)/shard_map/all_gather | solution.py:66
  283.5 7.5 %copy.44 = bf16[16,448,304]{1,0,2:T(8,128)(2,1)} copy(bf16[16,448,304]{1,2,0:T(8,128)(2,1)} %all-gather.15.cloned.1.call-done) | data formatting | bytes 8716288 | tf_op jit(solution)/shard_map/all_gather | solution.py:66
  291.0 9.0 %reshape.98 = bf16[7168,304]{0,1:T(8,128)(2,1)} reshape(bf16[16,448,304]{1,0,2:T(8,128)(2,1)} %copy.44) | data formatting | bytes 8716288
  300.0 43.3 %all-gather.13.cloned.1.call-done = bf16[16,448,304]{1,2,0:T(8,128)(2,1)} async-done(((bf16[1,448,304]{1,2,0:T(8,128)(2,1)}), bf16[16,448,304]{1,2,0:T(8,128)(2,1)}) %all-gather.13.cloned.1.call-update) | async-done | bytes 4358160 | tf_op jit(solution)/shard_map/all_gather | solution.py:67
  343.4 7.5 %copy.43 = bf16[16,448,304]{1,0,2:T(8,128)(2,1)} copy(bf16[16,448,304]{1,2,0:T(8,128)(2,1)} %all-gather.13.cloned.1.call-done) | data formatting | bytes 8716288 | tf_op jit(solution)/shard_map/all_gather | solution.py:67
  350.9 9.1 %reshape.96 = bf16[7168,304]{0,1:T(8,128)(2,1)} reshape(bf16[16,448,304]{1,0,2:T(8,128)(2,1)} %copy.43) | data formatting | bytes 8716288
  360.0 3.7 fusion.35
  363.7 3.7 fusion.36
  374.6 4.9 fusion.2
  379.5 7.4 %copy.56 = bf16[7168,304]{1,0:T(8,128)(2,1)} copy(bf16[7168,304]{0,1:T(8,128)(2,1)} %fusion.2) | data formatting | bytes 8716288
  390.2 7.5 %copy.54 = bf16[7168,304]{1,0:T(8,128)(2,1)} copy(bf16[7168,304]{0,1:T(8,128)(2,1)} %fusion.1) | data formatting | bytes 8716288
  401.1 7.5 %copy.52 = bf16[7168,304]{1,0:T(8,128)(2,1)} copy(bf16[7168,304]{0,1:T(8,128)(2,1)} %fusion) | data formatting | bytes 8716288
  420.2 89.3 %reduce-scatter.17.cloned.1.call-done = bf16[448,304]{1,0:T(8,128)(2,1)} async-done(((bf16[7168,304]{1,0:T(8,128)(2,1)}), bf16[448,304]{1,0:T(8,128)(2,1)}) %reduce-scatter.17.cloned.1.call-update) | async-done | bytes 272400
  510.6 88.2 %reduce-scatter.15.cloned.1.call-done = bf16[448,304]{1,0:T(8,128)(2,1)} async-done(((bf16[7168,304]{1,0:T(8,128)(2,1)}), bf16[448,304]{1,0:T(8,128)(2,1)}) %reduce-scatter.15.cloned.1.call-update) | async-done | bytes 272400
  601.5 86.2 %reduce-scatter.13.cloned.1.call-done = bf16[448,304]{1,0:T(8,128)(2,1)} async-done(((bf16[7168,304]{1,0:T(8,128)(2,1)}), bf16[448,304]{1,0:T(8,128)(2,1)}) %reduce-scatter.13.cloned.1.call-update) | async-done | bytes 272400
  (98 shorter events, 61.5 us)
Async XLA Ops:
  7.2 166.2 %copy-start = (bf16[1,192,7168]{2,1,0:T(8,128)(2,1)S(1)}, bf16[1,192,7168]{2,1,0:T(8,128)(2,1)}, u32[]{:S(2)}) copy-start(bf16[1,192,7168]{2,1,0:T(8,128)(2,1)} %param.17) | copy-start | bytes 8257540
  7.2 50.7 %all-gather.9.cloned.1.call-start = ((), (), s32[]{:S(2)}) async-start(), calls=%async_computation.7 | async-start | bytes 2064384 | tf_op jit(solution)/shard_map/all_gather | solution.py:63
  7.9 119.9 %all-gather.11.cloned.1.call-start = ((), (), s32[]{:S(2)}) async-start(), calls=%async_computation.8 | async-start | bytes 2064384 | tf_op jit(solution)/shard_map/all_gather | solution.py:62
  8.7 213.3 %all-gather.17.cloned.1.call-start = ((), (), s32[]{:S(2)}) async-start(), calls=%async_computation.12 | async-start | bytes 5292032 | tf_op jit(solution)/shard_map/all_gather | solution.py:65
  9.4 274.1 %all-gather.15.cloned.1.call-start = ((), (), s32[]{:S(2)}) async-start(), calls=%async_computation.11 | async-start | bytes 5292032 | tf_op jit(solution)/shard_map/all_gather | solution.py:66
  10.0 333.4 %all-gather.13.cloned.1.call-start = ((), (), s32[]{:S(2)}) async-start(), calls=%async_computation.10 | async-start | bytes 5292032 | tf_op jit(solution)/shard_map/all_gather | solution.py:67
  61.9 70.0 %all-to-all-start = ((bf16[16,6,7168]{2,1,0:T(8,128)(2,1)}), bf16[16,6,7168]{2,1,0:T(8,128)(2,1)}, u32[]{:S(2)}, u32[]{:S(2)}) async-start(bf16[16,6,7168]{2,1,0:T(8,128)(2,1)} %copy.49), calls=%async_computation | async-start | bytes 3670016 | tf_op jit(solution)/shard_map/all_to_all | solution.py:122
  131.9 38.9 %all-to-all-start.1 = ((bf16[16,6,7168]{2,1,0:T(8,128)(2,1)}), bf16[16,6,7168]{2,1,0:T(8,128)(2,1)}, u32[]{:S(2)}, u32[]{:S(2)}) async-start(bf16[16,6,7168]{2,1,0:T(8,128)(2,1)} %copy.50), calls=%async_computation.1 | async-start | bytes 3670016 | tf_op jit(solution)/shard_map/all_to_all | solution.py:121
  140.6 277.8 %reduce-scatter.11.cloned.1.call-start = ((), (), s32[]{:S(2)}) async-start(), calls=%async_computation.9 | async-start | bytes 2064384 | tf_op jit(solution)/shard_map/reduce_scatter | solution.py:150
  173.3 2.5 copy-start.3
  173.3 2.6 copy-start.10
  175.9 2.8 copy-start.11
  350.9 9.1 %copy-start.2 = (bf16[128,7168]{1,0:T(8,128)(2,1)S(1)}, bf16[128,7168]{1,0:T(8,128)(2,1)}, u32[]{:S(2)}) copy-start(bf16[128,7168]{1,0:T(8,128)(2,1)} %all-gather.11.cloned.1.call-done) | copy-start | bytes 5505028
  360.0 7.4 %copy-start.6 = (bf16[128,7168]{1,0:T(8,128)(2,1)S(1)}, bf16[128,7168]{1,0:T(8,128)(2,1)}, u32[]{:S(2)}) copy-start(bf16[128,7168]{1,0:T(8,128)(2,1)} %all-gather.9.cloned.1.call-done) | copy-start | bytes 5505028
  360.0 8.7 %slice-start = ((s8[4358144]{0:T(1024)(128)(4,1)}), s8[4194304]{0:T(1024)(128)(4,1)S(1)}, s32[]{:S(2)}) async-start(s8[4358144]{0:T(1024)(128)(4,1)} %bitcast.79), calls=%async_computation.16 | async-start | bytes 8388608
  363.7 3.7 copy-start.5
  363.7 5.0 slice-start.1
  368.7 3.3 copy-start.7
  374.5 134.9 %reduce-scatter.17.cloned.1.call-start = ((), (), s32[]{:S(2)}) async-start(), calls=%async_computation.15 | async-start | bytes 5849088
  386.9 211.9 %reduce-scatter.15.cloned.1.call-start = ((), (), s32[]{:S(2)}) async-start(), calls=%async_computation.14 | async-start | bytes 5849088
  397.7 289.9 %reduce-scatter.13.cloned.1.call-start = ((), (), s32[]{:S(2)}) async-start(), calls=%async_computation.13 | async-start | bytes 5849088
  412.4 2.4 copy-start.9
  414.8 3.7 copy-start.12
  414.8 274.8 %copy-start.1 = (bf16[1,192,7168]{2,1,0:T(8,128)(2,1)S(1)}, bf16[1,192,7168]{2,1,0:T(8,128)(2,1)}, u32[]{:S(2)}) copy-start(bf16[1,192,7168]{2,1,0:T(8,128)(2,1)} %param.17) | copy-start | bytes 8257540
  (4 other events, 7.0 us)
Sparse Core Ops, SparseCore 0:
  9.7 48.1 all-gather.8
  59.5 68.3 all-gather.10
  130.3 88.1 all-gather.16
  220.7 62.7 all-gather.14
  285.8 57.5 all-gather.12
  374.6 43.7 reduce-scatter.10
  422.6 86.8 reduce-scatter.16
  514.1 84.6 reduce-scatter.14
  602.9 84.7 reduce-scatter.12
where the time goes:
time: 698 us; the launch traced here: 696 us
  waiting for transfers between devices  484 us (69%)
  local copies, waits for them, and re-layouts  92.8 us (13%)
  matrix products  45.8 us (7%)
  blocking collectives  34.4 us (5%)
  starting transfers between devices  19.2 us (3%)
  between operations  14.1 us (2%)
    unnamed x12, waiting for transfers between devices  267 us
    unnamed x44, local copies, waits for them, and re-layouts  59 us
    all_gather x1, waiting for transfers between devices, per_device(): lax.all_gather(tokens, 'tp', axis=0, tiled=True)  55.9 us
    all_gather x1, waiting for transfers between devices, per_device(): full_up = lax.all_gather(dense_up, 'ep', axis=0, tiled=True)  45.2 us
    all_gather x1, waiting for transfers between devices, per_device(): lax.all_gather(cotangent, 'tp', axis=0, tiled=True)  43.6 us
    all_gather x1, waiting for transfers between devices, per_device(): full_down = lax.all_gather(dense_down, 'ep', axis=1, tiled=True)  43.3 us
    all_to_all x1, blocking collectives, per_device(): lax.all_to_all(back_rows.reshape(ep_count, capacity, width).astype(jnp.bf...  34.4 us
    all_to_all x1, waiting for transfers between devices, per_device(): lax.all_to_all(send_rows, 'ep', split_axis=0, concat_axis=0, tiled=True)  27.4 us
  transfers between devices with their start and end apart: 11, of which 9 were waited for; matrix products, arithmetic and copies ran while one was open for 16% of the time, Pallas kernels for 0%

commit v1 on v0

v1 whole, which is shorter than its diff:
```python
import functools
import math

import jax
import jax.numpy as jnp
from jax import lax
from jax.experimental import pallas as pl
from jax.experimental.pallas import tpu as pltpu
from jax.sharding import PartitionSpec as P

MESH = pl.DeviceIdType.MESH
F32 = jnp.float32
BF16 = jnp.bfloat16

NE, NT = 16, 8
GROUP, CAP = 128, 6
SLOTS = NE * CAP
HALF_SLOTS = SLOTS // 2
COVER = 512
FFB = 304
HID = 192


def dot_nt(a, b):
    return lax.dot_general(a, b, (((1,), (1,)), ((), ())), preferred_element_type=F32)


def dot_nn(a, b):
    return lax.dot_general(a, b, (((1,), (0,)), ((), ())), preferred_element_type=F32)


def dot_tn(a, b):
    return lax.dot_general(a, b, (((0,), (0,)), ((), ())), preferred_element_type=F32)


def unit_grads(gate_pre, up_pre, d_hidden):
    sigmoid_gate = jax.nn.sigmoid(gate_pre)
    activated = gate_pre * sigmoid_gate
    hidden = (activated * up_pre).astype(BF16)
    d_gate = (d_hidden * up_pre * sigmoid_gate * (1.0 + gate_pre * (1.0 - sigmoid_gate))).astype(BF16)
    d_up = (d_hidden * activated).astype(BF16)
    return hidden, d_gate, d_up


def cover_at(i):
    return pl.multiple_of(896 * (i // 2) + 384 * (i % 2), 128)


def kernel(
    scale_dense,
    tok, cot, route, wt, eg, eu, ed,
    gtok, gdense, eact, erows,
    xy, rr, part, c0r, x1r, x2r, z2r, hb, sel, sprob, ms, mr, we, eacc, bs, rb, dx, y1r, y2r, e2r, fs, fb, gacc,
    wsem, a_s, a_r, r_s, r_r, b_s, b_r, c0_s, c0_rs, c1_s, c1_rs, c2_s, c2_rs, d_s, d_r, m_s, m_r, e_s, e_r, f_s, f_r, osem,
):
    ep, tp = lax.axis_index("ep"), lax.axis_index("tp")
    x, zh, c = ep // 4, (ep // 2) % 2, ep % 2
    y, zl = tp // 2, tp % 2
    xp, xm, xo = (x + 1) % 4, (x + 3) % 4, (x + 2) % 4
    yp, ym, yo = (y + 1) % 4, (y + 3) % 4, (y + 2) % 4
    to_xp, to_xm = (ep + 4) % 16, (ep + 12) % 16
    dev_xp, dev_xm = (to_xp, tp), (to_xm, tp)
    dev_zh = ((x * 2 + 1 - zh) * 2 + c, tp)
    dev_core = ((x * 2 + zh) * 2 + 1 - c, tp)
    dev_yp, dev_ym = (ep, yp * 2 + zl), (ep, ym * 2 + zl)
    dev_zl = (ep, y * 2 + 1 - zl)

    def rc(src, dst, s, r, dev):
        return pltpu.make_async_remote_copy(
            src_ref=src, dst_ref=dst, send_sem=s, recv_sem=r, device_id=dev, device_id_type=MESH
        )

    def got(ref, r):
        rc(ref, ref, r, r, dev_core).wait_recv()

    def sent(ref, s):
        rc(ref, ref, s, s, dev_core).wait_send()

    loads = [pltpu.make_async_copy(w, we.at[n], wsem.at[n]) for n, w in enumerate((eg, eu, ed))]
    for w in loads:
        w.start()

    barrier = pltpu.get_barrier_semaphore()

    @pl.loop(1, NE)
    def _(k):
        pl.semaphore_signal(barrier, inc=1, device_id=((ep + k) % NE, tp), device_id_type=MESH)

    for d in (dev_yp, dev_ym, dev_zl):
        pl.semaphore_signal(barrier, inc=1, device_id=d, device_id_type=MESH)
    pl.semaphore_wait(barrier, NE - 1 + 3)

    srcs = (tok, cot)
    for a in range(2):

        @pl.loop(1, NE)
        def _(k):
            j = (ep + k) % NE
            rc(srcs[a].at[:, pl.ds(cover_at(j), COVER)], xy.at[a, ep, y, zl], a_s.at[a, k], a_r.at[a, k], (j, tp)).start()
            if a == 0:
                rc(route, rr.at[ep], r_s.at[k], r_r.at[k], (j, tp)).start()

        xy[a, ep, y, zl] = srcs[a][:, pl.ds(cover_at(ep), COVER)]
    rr[ep] = route[...]

    def blk(a, yy, zz):
        return xy.at[a, :, yy, zz]

    def lo(a, yy, zz):
        return xy.at[a, 0:8, yy, zz]

    def hi(a, yy, zz):
        return xy.at[a, 8:16, yy, zz]

    def send_b(a, n, ref, dev):
        rc(ref, ref, b_s.at[a, n], b_r.at[a, n], dev).start()

    for a in range(2):

        @pl.loop(1, NE)
        def _(k):
            i = (ep + NE - k) % NE
            got(xy.at[a, i, y, zl], a_r.at[a, k])

        send_b(a, 0, blk(a, y, zl), dev_zl)
        send_b(a, 1, blk(a, y, zl), dev_yp)
        send_b(a, 2, blk(a, y, zl), dev_ym)

    @pl.loop(1, NE)
    def _(k):
        got(rr.at[(ep + NE - k) % NE], r_r.at[k])

    base = ((tp // 2) * (2 * NE * HALF_SLOTS // 2)).astype(F32)
    for h in range(2):
        sprob[h] = jnp.zeros((NE * HALF_SLOTS, 128), F32)

        @pl.loop(0, 8)
        def _(gl):
            row = rr[h * 8 + gl]
            ids = lax.broadcasted_iota(jnp.int32, (NE * HALF_SLOTS, 128), 0).astype(F32)
            first = ids == (row[0:1] - base)
            second = ids == (row[1:2] - base)
            sel[h, :, pl.ds(pl.multiple_of(gl * 128, 128), 128)] = jnp.where(first | second, 1.0, 0.0).astype(BF16)
            sprob[h] += jnp.where(first, row[2:3], 0.0) + jnp.where(second, row[3:4], 0.0)

        sprob[h] = jnp.broadcast_to(jnp.sum(sprob[h], axis=1, keepdims=True), (NE * HALF_SLOTS, 128))

    def finish_b(a):
        got(blk(a, y, 1 - zl), b_r.at[a, 0])
        send_b(a, 3, blk(a, y, 1 - zl), dev_yp)
        send_b(a, 4, blk(a, y, 1 - zl), dev_ym)
        got(blk(a, ym, zl), b_r.at[a, 1])
        send_b(a, 5, lo(a, ym, zl), dev_yp)
        got(blk(a, yp, zl), b_r.at[a, 2])
        send_b(a, 6, hi(a, yp, zl), dev_ym)
        got(blk(a, ym, 1 - zl), b_r.at[a, 3])
        send_b(a, 7, lo(a, ym, 1 - zl), dev_yp)
        got(blk(a, yp, 1 - zl), b_r.at[a, 4])
        send_b(a, 8, hi(a, yp, 1 - zl), dev_ym)

    def end_b(a):
        got(lo(a, yo, zl), b_r.at[a, 5])
        got(hi(a, yo, zl), b_r.at[a, 6])
        got(lo(a, yo, 1 - zl), b_r.at[a, 7])
        got(hi(a, yo, 1 - zl), b_r.at[a, 8])

    spans = ((0, 2), (2, 3))

    def products(a):
        k0, k1 = spans[a]

        @pl.loop(0, 8)
        def _(p):
            rows = xy[a, pl.ds(2 * p, 2)].reshape(2 * GROUP, COVER)
            for k in range(k0, k1):
                res = dot_nt(wt[k], rows).astype(BF16)
                part[2 * p, k] = res[:, :GROUP]
                part[2 * p + 1, k] = res[:, GROUP:]
            rc(part.at[2 * p + 1 - c, k0:k1], c0r.at[p, k0:k1], c0_s.at[a, p], c0_rs.at[a, p], dev_core).start()

    def at1(buf, n, k0, k1):
        return buf.at[n, k0:k1]

    def at2(buf, n, m, k0, k1):
        return buf.at[n, m, k0:k1]

    def add(dst, srcs_):
        total = dst[...].astype(F32)
        for s in srcs_:
            total = total + s[...].astype(F32)
        dst[...] = total.astype(BF16)

    def sum_core(a):
        k0, k1 = spans[a]

        @pl.loop(0, 8)
        def _(p):
            got(c0r.at[p, k0:k1], c0_rs.at[a, p])
            for k in range(k0, k1):
                add(c0r.at[p, k], [part.at[2 * p + c, k]])

    def c1_sends(a):
        k0, k1 = spans[a]
        q = lambda xx, zz: c0r.at[xx * 2 + zz, k0:k1]
        return [
            rc(q(xo, 0), at1(x1r, 0, k0, k1), c1_s.at[a, 0], c1_rs.at[a, 0], dev_xp),
            rc(q(xo, 1), at1(x1r, 1, k0, k1), c1_s.at[a, 1], c1_rs.at[a, 1], dev_xm),
            rc(q(xp, 1), at2(x2r, 0, 1, k0, k1), c1_s.at[a, 2], c1_rs.at[a, 2], dev_xp),
            rc(q(xm, 0), at2(x2r, 1, 0, k0, k1), c1_s.at[a, 3], c1_rs.at[a, 3], dev_xm),
            rc(q(xp, 0), at2(x2r, 0, 0, k0, k1), c1_s.at[a, 4], c1_rs.at[a, 4], dev_xp),
            rc(q(xm, 1), at2(x2r, 1, 1, k0, k1), c1_s.at[a, 5], c1_rs.at[a, 5], dev_xm),
        ]

    def c1_first(a):
        for s in c1_sends(a)[:4]:
            s.start()

    def c1_second(a):
        k0, k1 = spans[a]
        sends = c1_sends(a)
        sends[0].wait_recv()
        for k in range(k0, k1):
            add(c0r.at[xp * 2, k], [x1r.at[0, k]])
        sends[4].start()
        sends[1].wait_recv()
        for k in range(k0, k1):
            add(c0r.at[xm * 2 + 1, k], [x1r.at[1, k]])
        sends[5].start()

    def c2_send(a):
        k0, k1 = spans[a]
        return rc(c0r.at[x * 2 + 1 - zh, k0:k1], z2r.at[k0:k1], c2_s.at[a], c2_rs.at[a], dev_zh)

    def c1_third(a):
        k0, k1 = spans[a]
        sends = c1_sends(a)
        for n in (2, 3, 4, 5):
            sends[n].wait_recv()
        for zz in (1 - zh, zh):
            for k in range(k0, k1):
                add(c0r.at[x * 2 + zz, k], [x2r.at[0, zz, k], x2r.at[1, zz, k]])
            if zz is not zh:
                c2_send(a).start()

    def routed(a):
        @pl.loop(0, 4)
        def _(n):
            jj = (x + n) % 4
            for h in range(2):
                rows = xy[a, 8 * h : 8 * h + 8].reshape(8 * GROUP, COVER)
                at = pl.multiple_of(jj * 4 * HALF_SLOTS, 64)
                res = dot_nn(sel[h, pl.ds(at, 4 * HALF_SLOTS)], rows)
                if a == 1:
                    res = res * sprob[h, pl.ds(at, 4 * HALF_SLOTS), 0:1]
                ms[a, pl.ds(jj * 4, 4), HALF_SLOTS * h : HALF_SLOTS * (h + 1)] = res.astype(BF16).reshape(4, HALF_SLOTS, COVER)

            @pl.loop(0, 4)
            def _(m):
                j = jj * 4 + m

                @pl.when(j != ep)
                def _():
                    rc(ms.at[a, j], mr.at[a, ep], m_s.at[a, j], m_r.at[a, ep], (j, tp)).start()

                @pl.when(j == ep)
                def _():
                    mr[a, j] = ms[a, j]

    def got_routed(a):
        @pl.loop(1, NE)
        def _(k):
            i = (ep + k) % NE
            got(mr.at[a, i], m_r.at[a, i])

    finish_b(0)
    end_b(0)
    products(0)
    finish_b(1)
    sum_core(0)
    c1_first(0)
    routed(0)
    end_b(1)
    products(1)
    sum_core(1)
    c1_first(1)
    c1_second(0)
    c1_second(1)
    c1_third(0)
    c1_third(1)
    for a in range(2):
        k0, k1 = spans[a]
        got(z2r.at[k0:k1], c2_rs.at[a])
    mine = [c0r[x * 2 + zh, k].astype(F32) + z2r[k].astype(F32) for k in range(3)]
    hidden, d_gate, d_up = unit_grads(*mine)
    hb[ep, 0] = d_gate
    hb[ep, 1] = d_up
    hb[ep, 2] = hidden

    def h_at(xx, zz):
        return hb.at[(xx * 2 + zz) * 2 + c]

    def send_d(n, ref, dev):
        rc(ref, ref, d_s.at[n], d_r.at[n], dev).start()

    def to_core(n, ref):
        rc(ref, ref, d_s.at[8 + n], d_r.at[8 + n], dev_core).start()

    own = h_at(x, zh)
    send_d(0, own, dev_zh)
    send_d(1, own, dev_xp)
    send_d(2, own, dev_xm)
    to_core(0, own)
    routed(1)
    got(h_at(x, 1 - zh), d_r.at[0])
    send_d(3, h_at(x, 1 - zh), dev_xp)
    send_d(4, h_at(x, 1 - zh), dev_xm)
    to_core(1, h_at(x, 1 - zh))
    got(h_at(xm, zh), d_r.at[1])
    send_d(5, h_at(xm, zh), dev_xp)
    to_core(2, h_at(xm, zh))
    got(h_at(xp, zh), d_r.at[2])
    to_core(3, h_at(xp, zh))
    got(h_at(xm, 1 - zh), d_r.at[3])
    to_core(4, h_at(xm, 1 - zh))
    got(h_at(xp, 1 - zh), d_r.at[4])
    send_d(6, h_at(xp, 1 - zh), dev_xm)
    to_core(5, h_at(xp, 1 - zh))
    got(h_at(xo, zh), d_r.at[5])
    to_core(6, h_at(xo, zh))
    got(h_at(xo, 1 - zh), d_r.at[6])
    to_core(7, h_at(xo, 1 - zh))

    for a in range(2):
        got_routed(a)
    for w in loads:
        w.wait()
    for n, a in enumerate((0, 0, 1)):
        total = jnp.zeros((SLOTS, HID), F32)
        for p in range(8):
            total += dot_nt(mr[a, 2 * p], we[n, :, 896 * p : 896 * p + 512])
            total += dot_nt(mr[a, 2 * p + 1, :, 128:512], we[n, :, 896 * p + 512 : 896 * p + 896])
        eacc[n] = total
    hidden, d_gate, d_up = unit_grads(eacc[0], eacc[1], eacc[2])
    eact[0] = d_gate
    eact[1] = d_up
    eact[2] = hidden

    @pl.loop(0, 8)
    def _(n):
        p = (ep // 2 + n) % 8
        at = pl.multiple_of(896 * p, 128)
        g, u = eact[0], eact[1]
        bs[2 * p] = (dot_nn(g, we[0, :, pl.ds(at, 512)]) + dot_nn(u, we[1, :, pl.ds(at, 512)])).astype(BF16)
        at2_ = pl.multiple_of(896 * p + 512, 128)
        bs[2 * p + 1, :, 0:128] = jnp.zeros((SLOTS, 128), BF16)
        bs[2 * p + 1, :, 128:512] = (
            dot_nn(g, we[0, :, pl.ds(at2_, 384)]) + dot_nn(u, we[1, :, pl.ds(at2_, 384)])
        ).astype(BF16)

        for m in range(2):
            i = 2 * p + m

            @pl.when(i != ep)
            def _():
                rc(bs.at[i], rb.at[ep], m_s.at[2, i], m_r.at[2, ep], (i, tp)).start()

            @pl.when(i == ep)
            def _():
                rb[i] = bs[i]

    outs = []
    for a in range(2):
        for p in range(8):
            outs.append(
                pltpu.make_async_copy(mr.at[a, 2 * p], erows.at[a, :, 896 * p : 896 * p + 512], osem.at[a, 2 * p])
            )
            outs.append(
                pltpu.make_async_copy(
                    mr.at[a, 2 * p + 1, :, 128:512], erows.at[a, :, 896 * p + 512 : 896 * p + 896], osem.at[a, 2 * p + 1]
                )
            )
    for o in outs:
        o.start()

    order = ((x, zh), (x, 1 - zh), (xm, zh), (xp, zh), (xm, 1 - zh), (xp, 1 - zh), (xo, zh), (xo, 1 - zh))
    for n, (xx, zz) in enumerate(order):
        got(hb.at[(xx * 2 + zz) * 2 + 1 - c], d_r.at[8 + n])

    got_routed_back = lambda: [got(rb.at[(ep + k) % NE], m_r.at[2, (ep + k) % NE]) for k in range(1, NE)]
    got_routed_back()
    for h in range(2):
        back = rb[:, HALF_SLOTS * h : HALF_SLOTS * (h + 1)].reshape(NE * HALF_SLOTS, COVER)

        @pl.loop(0, 4)
        def _(n):
            g = 8 * h + 2 * n
            s = sel[h, :, pl.ds(pl.multiple_of(n * 256, 256), 256)]
            total = dot_tn(s, back)
            for k in range(2):
                both = jnp.concatenate([hb[g, k], hb[g + 1, k]], axis=1)
                total = total + dot_tn(both, wt[k])
            dx[pl.ds(g, 2)] = total.astype(BF16).reshape(2, 4, 2, 16, COVER)

    def e_sends():
        return [
            rc(dx.at[0:8, yo], y1r.at[0], e_s.at[0], e_r.at[0], dev_yp),
            rc(dx.at[8:16, yo], y1r.at[1], e_s.at[1], e_r.at[1], dev_ym),
            rc(dx.at[8:16, yp], y2r.at[0, 8:16], e_s.at[2], e_r.at[2], dev_yp),
            rc(dx.at[0:8, ym], y2r.at[1, 0:8], e_s.at[3], e_r.at[3], dev_ym),
            rc(dx.at[0:8, yp], y2r.at[0, 0:8], e_s.at[4], e_r.at[4], dev_yp),
            rc(dx.at[8:16, ym], y2r.at[1, 8:16], e_s.at[5], e_r.at[5], dev_ym),
            rc(dx.at[:, y, 1 - zl], e2r, e_s.at[6], e_r.at[6], dev_zl),
        ]

    es = e_sends()
    for s in es[:4]:
        s.start()

    for k in range(3):
        gacc[...] = jnp.zeros((FFB, COVER), F32)

        @pl.loop(0, 4)
        def _(n):
            left = jnp.concatenate([hb[4 * n + m, k] for m in range(4)], axis=1)
            rows = xy[0 if k < 2 else 1, pl.ds(4 * n, 4)].reshape(4 * GROUP, COVER)
            gacc[...] += dot_nn(left, rows)

        gdense[k] = (gacc[...] * scale_dense).astype(BF16)

    es[0].wait_recv()
    add(dx.at[0:8, yp], [y1r.at[0]])
    es[4].start()
    es[1].wait_recv()
    add(dx.at[8:16, ym], [y1r.at[1]])
    es[5].start()
    for n in (2, 3, 4, 5):
        es[n].wait_recv()
    add(dx.at[:, y, 1 - zl], [y2r.at[0, :, 1 - zl], y2r.at[1, :, 1 - zl]])
    es[6].start()
    add(dx.at[:, y, zl], [y2r.at[0, :, zl], y2r.at[1, :, zl]])
    es[6].wait_recv()
    fs[...] = (dx[:, y, zl].astype(F32) + e2r[...].astype(F32)).astype(BF16)

    @pl.loop(1, NE)
    def _(k):
        j = (ep + k) % NE
        rc(fs.at[j], fb.at[ep], f_s.at[k], f_r.at[k], (j, tp)).start()

    fb[ep] = fs[ep]

    @pl.loop(1, NE)
    def _(k):
        got(fb.at[(ep + NE - k) % NE], f_r.at[k])

    for p in range(8):
        even, odd = fb[2 * p].astype(F32), fb[2 * p + 1].astype(F32)
        at = 896 * p
        gtok[:, at : at + 384] = (cot[:, at : at + 384].astype(F32) + even[:, 0:384]).astype(BF16)
        gtok[:, at + 384 : at + 512] = (
            cot[:, at + 384 : at + 512].astype(F32) + even[:, 384:512] + odd[:, 0:128]
        ).astype(BF16)
        gtok[:, at + 512 : at + 896] = (cot[:, at + 512 : at + 896].astype(F32) + odd[:, 128:512]).astype(BF16)

    for o in outs:
        o.wait()

    @pl.loop(1, NE)
    def _(k):
        j = (ep + k) % NE
        for a in range(2):
            sent(xy.at[a, ep, y, zl], a_s.at[a, k])
            sent(ms.at[a, j], m_s.at[a, j])
        sent(bs.at[j], m_s.at[2, j])
        sent(route, r_s.at[k])
        sent(fs.at[j], f_s.at[k])

    for a in range(2):
        for n in range(5):
            sent(blk(a, y, zl), b_s.at[a, n])
        for n in range(5, 9):
            sent(lo(a, y, zl), b_s.at[a, n])
        k0, k1 = spans[a]

        @pl.loop(0, 8)
        def _(p):
            sent(c0r.at[p, k0:k1], c0_s.at[a, p])

        for s in c1_sends(a):
            s.wait_send()
        c2_send(a).wait_send()

    @pl.loop(0, 7)
    def _(n):
        sent(own, d_s.at[n])

    @pl.loop(8, 16)
    def _(n):
        sent(own, d_s.at[n])

    for s in es:
        s.wait_send()


def exchange(tokens, cotangent, route, wt, eg, eu, ed, scale_dense):
    vm = lambda shape, dt=BF16: pltpu.VMEM(shape, dt)
    dma = lambda *shape: pltpu.SemaphoreType.DMA(shape)
    width = tokens.shape[1]
    vspec = pl.BlockSpec(memory_space=pltpu.VMEM)
    hspec = pl.BlockSpec(memory_space=pl.ANY)
    return pl.pallas_call(
        functools.partial(kernel, scale_dense),
        name="exchange",
        out_shape=(
            jax.ShapeDtypeStruct(tokens.shape, BF16),
            jax.ShapeDtypeStruct((3, FFB, COVER), BF16),
            jax.ShapeDtypeStruct((3, SLOTS, HID), BF16),
            jax.ShapeDtypeStruct((2, SLOTS, width), BF16),
        ),
        in_specs=[vspec] * 4 + [hspec] * 3,
        out_specs=(vspec, vspec, vspec, hspec),
        scratch_shapes=[
            vm((2, NE, 4, 2, 16, COVER)),
            vm((NE, 8, 128), F32),
            vm((NE, 3, FFB, GROUP)),
            vm((8, 3, FFB, GROUP)),
            vm((2, 3, FFB, GROUP)),
            vm((2, 2, 3, FFB, GROUP)),
            vm((3, FFB, GROUP)),
            vm((NE, 3, FFB, GROUP)),
            vm((2, NE * HALF_SLOTS, 8 * GROUP)),
            vm((2, NE * HALF_SLOTS, 128), F32),
            vm((2, NE, SLOTS, COVER)),
            vm((2, NE, SLOTS, COVER)),
            vm((3, HID, width)),
            vm((3, SLOTS, HID), F32),
            vm((NE, SLOTS, COVER)),
            vm((NE, SLOTS, COVER)),
            vm((NE, 4, 2, 16, COVER)),
            vm((2, 8, 2, 16, COVER)),
            vm((2, NE, 2, 16, COVER)),
            vm((NE, 16, COVER)),
            vm((NE, 16, COVER)),
            vm((NE, 16, COVER)),
            vm((FFB, COVER), F32),
            dma(3),
            dma(2, NE), dma(2, NE),
            dma(NE), dma(NE),
            dma(2, 9), dma(2, 9),
            dma(2, 8), dma(2, 8),
            dma(2, 6), dma(2, 6),
            dma(2), dma(2),
            dma(16), dma(16),
            dma(3, NE), dma(3, NE),
            dma(7), dma(7),
            dma(NE), dma(NE),
            dma(2, NE),
        ],
        compiler_params=pltpu.CompilerParams(
            collective_id=0, has_side_effects=True, vmem_limit_bytes=60 * 1024 * 1024
        ),
    )(tokens, cotangent, route, wt, eg, eu, ed)


def product_left(left, right):
    return lax.dot_general(left, right, (((0,), (0,)), ((), ())), preferred_element_type=F32)


def per_device(
    tokens, cotangent, route_ids, route_probs, dense_gate, dense_up, dense_down, expert_gate, expert_up, expert_down
):
    ep = lax.axis_index("ep")
    core = ep % 2
    total_tokens = NE * GROUP
    scale_dense = 1.0 / math.sqrt(total_tokens)
    scale_expert = math.sqrt(NE * NT // 2 / (2.0 * total_tokens))

    flat = route_ids.reshape(-1)
    place = jnp.arange(flat.shape[0])
    rank = jnp.sum((flat[:, None] == flat[None, :]) & (place[None, :] < place[:, None]), axis=1, dtype=jnp.int32)
    code = (flat % 4) * (NE * HALF_SLOTS) + (flat // 4) * HALF_SLOTS + (ep % 8) * CAP + rank
    code = code.reshape(GROUP, 2).astype(F32).T
    route = jnp.concatenate([code, route_probs.T, jnp.zeros((4, GROUP), F32)], axis=0)

    stacked = jnp.stack([dense_gate.T, dense_up.T, dense_down])
    pad = COVER - stacked.shape[2]
    wt = jnp.where(
        core == 0, jnp.pad(stacked, ((0, 0), (0, 0), (0, pad))), jnp.pad(stacked, ((0, 0), (0, 0), (pad, 0)))
    )
    gtok, gdense, eact, erows = exchange(
        tokens, cotangent, route, wt, expert_gate[0], expert_up[0], expert_down[0], scale_dense
    )
    gdense = jnp.where(core == 0, gdense[:, :, : COVER - pad], gdense[:, :, pad:])
    grads = [
        (product_left(eact[n], erows[a]) * scale_expert).astype(BF16)[None] for n, a in enumerate((0, 0, 1))
    ]
    return (gtok, gdense[0].T, gdense[1].T, gdense[2], *grads)


def solution(mesh):
    return jax.shard_map(
        per_device,
        mesh=mesh,
        in_specs=(
            P(("ep", "tp"), None),
            P(("ep", "tp"), None),
            P("ep", None),
            P("ep", None),
            P("ep", "tp"),
            P("ep", "tp"),
            P("tp", "ep"),
            P(("ep", "tp"), None, None),
            P(("ep", "tp"), None, None),
            P(("ep", "tp"), None, None),
        ),
        out_specs=(
            P(("ep", "tp"), None),
            P("ep", "tp"),
            P("ep", "tp"),
            P("tp", "ep"),
            P(("ep", "tp"), None, None),
            P(("ep", "tp"), None, None),
            P(("ep", "tp"), None, None),
        ),
        check_vma=False,
    )
```

time: 698 us -> 216 us (0.31)
  waiting for transfers between devices: 484 us -> 0 us
  Pallas kernels: 0 us -> 198 us
  local copies, waits for them, and re-layouts: 92.8 us -> 2.85 us
  matrix products: 45.8 us -> 7.3 us
  blocking collectives: 34.4 us -> 0 us
  starting transfers between devices: 19.2 us -> 0 us
  between operations: 14.1 us -> 0.71 us
    unnamed x12 -> x0, waiting for transfers between devices: 267 us -> none
    pallas_call x0 -> x1, Pallas kernels: none -> 198 us  [exchange(): pl.pallas_call(functools.partial(kernel, scale_dense), name='exchange', o...]
    all_gather x5 -> x0, waiting for transfers between devices: 188 us -> none  [the longest x1 55.9 us: per_device(): lax.all_gather(tokens, 'tp', axis=0, tiled=True)]
    unnamed x44 -> x8, local copies, waits for them, and re-layouts: 59 us -> 1.48 us
    all_to_all x1 -> x0, blocking collectives: 34.4 us -> none  [per_device(): lax.all_to_all(back_rows.reshape(ep_count, capacity, width).astype(jnp.bf...]
    all_to_all x2 -> x0, waiting for transfers between devices: 27.4 us -> none  [the longest x1 27.4 us: per_device(): lax.all_to_all(send_rows, 'ep', split_axis=0, concat_axis=0, tiled=True)]
    dot_general x13 -> x0, matrix products: 27 us -> none  [the longest x4 9.5 us: product(): return jnp.dot(left, right, preferred_element_type=jnp.float32)]
    all_gather x3 -> x0, local copies, waits for them, and re-layouts: 22.4 us -> none  [the longest x1 7.5 us: per_device(): full_up = lax.all_gather(dense_up, 'ep', axis=0, tiled=True)]
  transfers between devices with their start and end apart: 11 -> 0, of which waited for: 9 -> 0; matrix products, arithmetic and copies ran while one was open for 16% -> 0% of each run, Pallas kernels for 0% -> 0%
where the time goes in v1:
time: 216 us
  Pallas kernels  198 us (92%)
  matrix products  7.3 us (3%)
  other arithmetic  7.16 us (3%)
  local copies, waits for them, and re-layouts  2.85 us (1%)
    pallas_call x1, Pallas kernels, exchange(): pl.pallas_call(functools.partial(kernel, scale_dense), name='exchange', o...  198 us
    dot_general x3, matrix products, product_left(): lax.dot_general(left, right, (((0,), (0,)), ((), ())), preferred_element_...  7.3 us

profile of v1, /device:TPU:1, one launch (start us, length us, event | category | flops | bytes accessed | tf_op | source)
XLA Modules:
  0.0 215.7 jit_solution(18302454841780400370)
XLA Ops:
  0.7 0.1 pad.15.clone
  0.7 0.8 copy.19
  1.5 0.1 eq.24
  1.7 0.2 convert_reduce_fusion
  1.8 0.1 reduce_sum.12
  2.0 0.1 copy.20
  2.1 0.7 convert_bitcast_fusion
  2.8 1.3 maximum_maximum_fusion.route
  4.1 1.3 pad_maximum_fusion
  5.4 1.7 pad_select_fusion.wt
  7.1 197.6 %exchange.1 = (bf16[16,7168]{1,0:T(8,128)(2,1)}, bf16[3,304,512]{2,1,0:T(8,128)(2,1)}, bf16[3,96,192]{2,1,0:T(8,128)(2,1)}, bf16[2,96,7168]{2,1,0:T(8,128)(2,1)}) custom-call(bf16[16,7168]{1,0:T(8,128)(2,1)} %tok.1, bf16[16,7168]{1,0:T(8,128)(2,1)} %cot.1, f32[8,128]{1,0:T(8,128)} %maximum_maximum_fusion.route, bf16[3,304,512]{2,1,0:T(8,128)(2,1)} %pad_select_fusion.wt, ...), custom_call_target="tpu_custom_call" | custom-call | tf_op jit(solution)/shard_map/exchange/pallas_call | solution.py:510
  204.7 0.0 copy-start
  204.8 0.0 copy-start.2
  204.8 1.9 slice_select_fusion
  206.7 0.9 slice_bitcast_fusion
  207.7 0.0 copy-done
  207.7 0.0 copy-done.2
  207.7 2.4 %fusion.3 = bf16[1,192,7168]{2,1,0:T(8,128)(2,1)} fusion(bf16[2,96,7168]{2,1,0:T(8,128)(2,1)S(1)} %copy-done, bf16[3,96,192]{2,1,0:T(8,128)(2,1)S(1)} %copy-done.2), kind=kOutput, calls=%fused_computation.6 | convolution fusion | flops 266993664 | bytes 4177920 | tf_op jit(solution)/shard_map/dot_general | solution.py:565
  210.1 2.4 %fusion.4 = bf16[1,192,7168]{2,1,0:T(8,128)(2,1)} fusion(bf16[2,96,7168]{2,1,0:T(8,128)(2,1)S(1)} %copy-done, bf16[3,96,192]{2,1,0:T(8,128)(2,1)S(1)} %copy-done.2), kind=kOutput, calls=%fused_computation.7 | convolution fusion | flops 266993664 | bytes 4177920 | tf_op jit(solution)/shard_map/dot_general | solution.py:565
  212.5 0.0 copy-start.1
  212.5 2.4 %fusion.5 = bf16[1,192,7168]{2,1,0:T(8,128)(2,1)} fusion(bf16[2,96,7168]{2,1,0:T(8,128)(2,1)S(1)} %copy-done, bf16[3,96,192]{2,1,0:T(8,128)(2,1)S(1)} %copy-done.2), kind=kOutput, calls=%fused_computation.8 | convolution fusion | flops 266993664 | bytes 4177920 | tf_op jit(solution)/shard_map/dot_general | solution.py:565
  215.0 0.0 copy-done.1
  215.0 0.7 copy.22
  (1 shorter events, 0.0 us)
Async XLA Ops:
  204.7 2.9 %copy-start = (bf16[2,96,7168]{2,1,0:T(8,128)(2,1)S(1)}, bf16[2,96,7168]{2,1,0:T(8,128)(2,1)}, u32[]{:S(2)}) copy-start(bf16[2,96,7168]{2,1,0:T(8,128)(2,1)} %get-tuple-element.14) | copy-start | bytes 8257540
  204.8 2.9 %copy-start.2 = (bf16[3,96,192]{2,1,0:T(8,128)(2,1)S(1)}, bf16[3,96,192]{2,1,0:T(8,128)(2,1)}, u32[]{:S(2)}) copy-start(bf16[3,96,192]{2,1,0:T(8,128)(2,1)} %get-tuple-element.13) | copy-start | bytes 331780
  212.5 2.4 %copy-start.1 = (bf16[16,7168]{1,0:T(8,128)(2,1)S(1)}, bf16[16,7168]{1,0:T(8,128)(2,1)}, u32[]{:S(2)}) copy-start(bf16[16,7168]{1,0:T(8,128)(2,1)} %get-tuple-element.25) | copy-start | bytes 688132

commit v2 on v1

v2 whole, which is shorter than its diff:
```python
import functools
import math

import jax
import jax.numpy as jnp
from jax import lax
from jax.experimental import pallas as pl
from jax.experimental.pallas import tpu as pltpu
from jax.sharding import PartitionSpec as P

MESH = pl.DeviceIdType.MESH
F32 = jnp.float32
BF16 = jnp.bfloat16

NE, NT = 16, 8
GROUP, CAP = 128, 6
SLOTS = NE * CAP
HALF_SLOTS = SLOTS // 2
COVER = 512
FFB = 304
HID = 192


def dot_nt(a, b):
    return lax.dot_general(a, b, (((1,), (1,)), ((), ())), preferred_element_type=F32)


def dot_nn(a, b):
    return lax.dot_general(a, b, (((1,), (0,)), ((), ())), preferred_element_type=F32)


def dot_tn(a, b):
    return lax.dot_general(a, b, (((0,), (0,)), ((), ())), preferred_element_type=F32)


def unit_grads(gate_pre, up_pre, d_hidden):
    sigmoid_gate = jax.nn.sigmoid(gate_pre)
    activated = gate_pre * sigmoid_gate
    hidden = (activated * up_pre).astype(BF16)
    d_gate = (d_hidden * up_pre * sigmoid_gate * (1.0 + gate_pre * (1.0 - sigmoid_gate))).astype(BF16)
    d_up = (d_hidden * activated).astype(BF16)
    return hidden, d_gate, d_up


def kernel(
    scale_dense,
    tok, cot, ids, probs, dgate, dup, ddown, eg, eu, ed,
    gtok, gdense, eact, erows,
    xy, route, rr, wt, part, c0r, x1r, x2r, z2r, hb, sel, sprob, ms, mr, we, eacc, bs, rb, dx, er, fs, fb, gacc,
    wsem, a_s, a_r, r_s, r_r, b_s, b_r, c0_s, c0_rs, c1_s, c1_rs, c2_s, c2_rs, d_s, d_r, m_s, m_r, e_s, e_r, f_s, f_r, k_s, k_r, osem,
):
    ep, tp = lax.axis_index("ep"), lax.axis_index("tp")
    x, zh, c = ep // 4, (ep // 2) % 2, ep % 2
    y, zl = tp // 2, tp % 2
    xo, xs, xr = (x + 2) % 4, (x + 1 + 2 * c) % 4, (x + 3 + 2 * c) % 4
    yo, ys, yr = (y + 2) % 4, (y + 1 + 2 * c) % 4, (y + 3 + 2 * c) % 4

    full, rest = slice(0, COVER), slice(128, COVER)

    def by_core(act):
        pl.when(c == 0)(lambda: act(full))
        pl.when(c == 1)(lambda: act(rest))

    def dev_x(xx):
        return ((xx * 2 + zh) * 2 + c, tp)

    def dev_y(yy):
        return (ep, yy * 2 + zl)

    dev_zh = ((x * 2 + 1 - zh) * 2 + c, tp)
    dev_core = ((x * 2 + zh) * 2 + 1 - c, tp)
    dev_zl = (ep, y * 2 + 1 - zl)

    def rc(src, dst, s, r, dev):
        return pltpu.make_async_remote_copy(
            src_ref=src, dst_ref=dst, send_sem=s, recv_sem=r, device_id=dev, device_id_type=MESH
        )

    def got(ref, r):
        rc(ref, ref, r, r, dev_core).wait_recv()

    def sent(ref, s):
        rc(ref, ref, s, s, dev_core).wait_send()

    def add(dst, srcs_):
        total = dst[...].astype(F32)
        for s in srcs_:
            total = total + s[...].astype(F32)
        dst[...] = total.astype(BF16)

    loads = [pltpu.make_async_copy(w, we.at[n], wsem.at[n]) for n, w in enumerate((eg, eu, ed))]
    for w in loads:
        w.start()

    @pl.when(c == 1)
    def _():
        rb[:, :, 0:128] = jnp.zeros((NE, SLOTS, 128), BF16)

    barrier = pltpu.get_barrier_semaphore()

    @pl.loop(1, NE)
    def _(k):
        pl.semaphore_signal(barrier, inc=1, device_id=((ep + k) % NE, tp), device_id_type=MESH)

    @pl.loop(1, NT)
    def _(k):
        pl.semaphore_signal(barrier, inc=1, device_id=(ep, (tp + k) % NT), device_id_type=MESH)


    pl.semaphore_wait(barrier, NE - 1 + NT - 1)

    srcs = (tok, cot)

    def a_copy(a, k):
        j = (ep + k) % NE
        at = pl.multiple_of(896 * (j // 2) + 512 * (j % 2), 128)
        return lambda lanes: rc(
            srcs[a].at[:, pl.ds(at, lanes.stop - lanes.start)],
            xy.at[a, ep, y, zl, :, lanes], a_s.at[a, k], a_r.at[a, k], (j, tp),
        )

    def a_send(a):
        @pl.loop(1, NE)
        def _(k):
            pl.when((ep + k) % 2 == 0)(lambda: a_copy(a, k)(full).start())
            pl.when((ep + k) % 2 == 1)(lambda: a_copy(a, k)(rest).start())

        @pl.when(c == 0)
        def _():
            xy[a, ep, y, zl] = srcs[a][:, pl.ds(pl.multiple_of(896 * (ep // 2), 128), 512)]

        @pl.when(c == 1)
        def _():
            xy[a, ep, y, zl, :, 128:512] = srcs[a][:, pl.ds(pl.multiple_of(896 * (ep // 2) + 512, 128), 384)]

    a_send(0)

    before = lax.broadcasted_iota(jnp.int32, (GROUP, GROUP), 0) < lax.broadcasted_iota(jnp.int32, (GROUP, GROUP), 1)
    across = [jnp.broadcast_to(ids[k : k + 1, :].astype(F32), (GROUP, GROUP)) for k in range(2)]
    down = [jnp.transpose(m) for m in across]
    codes = []
    for k in range(2):
        rank = jnp.zeros((1, GROUP), F32)
        for m in down:
            rank = rank + jnp.sum(jnp.where(before & (m == across[k]), 1.0, 0.0), axis=0, keepdims=True)
        idk = ids[k : k + 1, :]
        group_at = (ep % 8) * CAP
        fixed = (idk & 3) * (NE * HALF_SLOTS) + (idk >> 2) * HALF_SLOTS + group_at
        codes.append(fixed.astype(F32) + rank)
    route[...] = jnp.concatenate([codes[0], codes[1], probs[...], jnp.zeros((4, GROUP), F32)], axis=0)

    @pl.loop(1, NE)
    def _(k):
        rc(route, rr.at[ep], r_s.at[k], r_r.at[k], ((ep + k) % NE, tp)).start()

    a_send(1)
    blank = jnp.zeros((FFB, COVER - 448), BF16)

    @pl.when(c == 0)
    def _():
        for k, w in enumerate((dgate, dup, ddown)):
            wt[k] = jnp.concatenate([w[...], blank], axis=1)

    @pl.when(c == 1)
    def _():
        for k, w in enumerate((dgate, dup, ddown)):
            wt[k] = jnp.concatenate([blank, w[...]], axis=1)

    rr[ep] = route[...]

    def got_a(a):
        @pl.loop(1, NE)
        def _(k):
            i = (ep + NE - k) % NE
            by_core(lambda lanes: got(xy.at[a, i, y, zl, :, lanes], a_r.at[a, k]))

    def send_b(a, h, n, yy, zz, dev):
        def act(lanes):
            ref = xy.at[a, 8 * h : 8 * h + 8, yy, zz, :, lanes]
            rc(ref, ref, b_s.at[2 * a + h, n], b_r.at[2 * a + h, n], dev).start()

        by_core(act)

    def got_b(a, h, n, yy, zz):
        by_core(lambda lanes: got(xy.at[a, 8 * h : 8 * h + 8, yy, zz, :, lanes], b_r.at[2 * a + h, n]))

    def sent_b(a, h, n):
        by_core(lambda lanes: sent(xy.at[a, 8 * h : 8 * h + 8, y, zl, :, lanes], b_s.at[2 * a + h, n]))

    def b_zero(a):
        for h in range(2):
            send_b(a, h, 0, y, zl, dev_zl)

    def b_first(a, h):
        send_b(a, h, 1, y, zl, dev_y(ys))
        send_b(a, h, 2, y, zl, dev_y(yr))

    def b_mid(a, h):
        got_b(a, h, 0, y, 1 - zl)
        send_b(a, h, 3, y, 1 - zl, dev_y(ys))
        send_b(a, h, 4, y, 1 - zl, dev_y(yr))

    def b_forward(a, h, second):
        if second:
            got_b(a, h, 3, yr, 1 - zl)
            send_b(a, h, 6, yr, 1 - zl, dev_y(ys))
        else:
            got_b(a, h, 1, yr, zl)
            send_b(a, h, 5, yr, zl, dev_y(ys))
            got_b(a, h, 2, ys, zl)

    def shared(a, h, at):
        return xy.at[a, 8 * h : 8 * h + 8, :, :, :, at : at + 128]

    def b_end(a, h):
        got_b(a, h, 5, yo, zl)
        got_b(a, h, 4, ys, 1 - zl)
        got_b(a, h, 6, yo, 1 - zl)

        @pl.when(c == 0)
        def _():
            rc(shared(a, h, 384), shared(a, h, 0), k_s.at[2 * a + h], k_r.at[2 * a + h], dev_core).start()

        @pl.when(c == 1)
        def _():
            got(shared(a, h, 0), k_r.at[2 * a + h])

    def slots():
        @pl.loop(1, NE)
        def _(k):
            got(rr.at[(ep + NE - k) % NE], r_r.at[k])

        base = ((tp // 2) * (NE * HALF_SLOTS)).astype(F32)
        for h in range(2):
            sprob[h] = jnp.zeros((NE * HALF_SLOTS, 128), F32)

            @pl.loop(0, 8)
            def _(gl):
                row = rr[h * 8 + gl]
                numbers = lax.broadcasted_iota(jnp.int32, (NE * HALF_SLOTS, 128), 0).astype(F32)
                first = numbers == (row[0:1] - base)
                second = numbers == (row[1:2] - base)
                sel[h, :, pl.ds(pl.multiple_of(gl * 128, 128), 128)] = jnp.where(first | second, 1.0, 0.0).astype(BF16)
                sprob[h] += jnp.where(first, row[2:3], 0.0) + jnp.where(second, row[3:4], 0.0)

            sprob[h] = jnp.broadcast_to(jnp.sum(sprob[h], axis=1, keepdims=True), (NE * HALF_SLOTS, 128))

    spans = ((0, 2), (2, 3))

    def products(a):
        k0, k1 = spans[a]

        @pl.loop(0, 8)
        def _(p):
            rows = xy[a, pl.ds(2 * p, 2)].reshape(2 * GROUP, COVER)
            for k in range(k0, k1):
                res = dot_nt(wt[k], rows).astype(BF16)
                part[2 * p, k] = res[:, :GROUP]
                part[2 * p + 1, k] = res[:, GROUP:]
            rc(
                part.at[2 * p + 1 - c, k0:k1], c0r.at[p // 2, p % 2, k0:k1], c0_s.at[a, p], c0_rs.at[a, p], dev_core
            ).start()

    def sum_core(a):
        k0, k1 = spans[a]

        @pl.loop(0, 8)
        def _(p):
            got(c0r.at[p // 2, p % 2, k0:k1], c0_rs.at[a, p])
            for k in range(k0, k1):
                add(c0r.at[p // 2, p % 2, k], [part.at[2 * p + c, k]])

    def c1_sends(a):
        k0, k1 = spans[a]
        q = lambda xx: c0r.at[xx, :, k0:k1]
        return [
            rc(q(xo), x1r.at[:, k0:k1], c1_s.at[a, 0], c1_rs.at[a, 0], dev_x(xs)),
            rc(q(xr), x2r.at[1, :, k0:k1], c1_s.at[a, 1], c1_rs.at[a, 1], dev_x(xr)),
            rc(q(xs), x2r.at[0, :, k0:k1], c1_s.at[a, 2], c1_rs.at[a, 2], dev_x(xs)),
        ]

    def c1_first(a):
        for s in c1_sends(a)[:2]:
            s.start()

    def c1_second(a):
        k0, k1 = spans[a]
        sends = c1_sends(a)
        sends[0].wait_recv()
        for zz in range(2):
            for k in range(k0, k1):
                add(c0r.at[xs, zz, k], [x1r.at[zz, k]])
        sends[2].start()

    def c2_send(a):
        k0, k1 = spans[a]
        return rc(c0r.at[x, 1 - zh, k0:k1], z2r.at[k0:k1], c2_s.at[a], c2_rs.at[a], dev_zh)

    def c1_third(a):
        k0, k1 = spans[a]
        sends = c1_sends(a)
        for n in (1, 2):
            sends[n].wait_recv()
        for n, zz in enumerate((1 - zh, zh)):
            for k in range(k0, k1):
                add(c0r.at[x, zz, k], [x2r.at[0, zz, k], x2r.at[1, zz, k]])
            if n == 0:
                c2_send(a).start()

    def rows_of(h):
        return slice(HALF_SLOTS * h, HALF_SLOTS * (h + 1))

    def m_copy(a, h, j, lanes):
        return rc(
            ms.at[a, j, rows_of(h), lanes], mr.at[a, ep, rows_of(h), lanes], m_s.at[2 * a + h, j], m_r.at[2 * a + h, ep], (j, tp)
        )

    def routed(a, h):
        @pl.loop(0, 4)
        def _(n):
            jj = (x + n) % 4
            rows = xy[a, 8 * h : 8 * h + 8].reshape(8 * GROUP, COVER)
            at = pl.multiple_of(jj * 4 * HALF_SLOTS, 64)
            res = dot_nn(sel[h, pl.ds(at, 4 * HALF_SLOTS)], rows)
            if a == 1:
                res = res * sprob[h, pl.ds(at, 4 * HALF_SLOTS), 0:1]
            ms[a, pl.ds(jj * 4, 4), rows_of(h)] = res.astype(BF16).reshape(4, HALF_SLOTS, COVER)

            @pl.loop(0, 4)
            def _(m):
                j = jj * 4 + m

                @pl.when((j != ep) & (c == 0))
                def _():
                    m_copy(a, h, j, full).start()

                @pl.when((j != ep) & (c == 1))
                def _():
                    m_copy(a, h, j, rest).start()

                @pl.when(j == ep)
                def _():
                    mr[a, j, rows_of(h)] = ms[a, j, rows_of(h)]

    def got_routed(a, h):
        @pl.loop(0, 8)
        def _(p):
            @pl.when(2 * p != ep)
            def _():
                got(mr.at[a, 2 * p, rows_of(h)], m_r.at[2 * a + h, 2 * p])

            @pl.when(2 * p + 1 != ep)
            def _():
                got(mr.at[a, 2 * p + 1, rows_of(h), rest], m_r.at[2 * a + h, 2 * p + 1])

    def expert_forward(h):
        for a in range(2):
            got_routed(a, h)
        if h == 0:
            for w in loads:
                w.wait()
        for n, a in enumerate((0, 0, 1)):
            total = jnp.zeros((HALF_SLOTS, HID), F32)
            for p in range(8):
                total += dot_nt(mr[a, 2 * p, rows_of(h)], we[n, :, 896 * p : 896 * p + 512])
                total += dot_nt(mr[a, 2 * p + 1, rows_of(h), rest], we[n, :, 896 * p + 512 : 896 * p + 896])
            eacc[n] = total
        hidden, d_gate, d_up = unit_grads(eacc[0], eacc[1], eacc[2])
        eact[0, rows_of(h)] = d_gate
        eact[1, rows_of(h)] = d_up
        eact[2, rows_of(h)] = hidden

    def back_copy(h, i, lanes):
        return rc(bs.at[i, rows_of(h), lanes], rb.at[ep, rows_of(h), lanes], m_s.at[4 + h, i], m_r.at[4 + h, ep], (i, tp))

    def expert_back(h):
        @pl.loop(0, 8)
        def _(n):
            p = (ep // 2 + n) % 8
            g, u = eact[0, rows_of(h)], eact[1, rows_of(h)]
            for m, lanes in enumerate((full, rest)):
                i = 2 * p + m
                wide = pl.ds(pl.multiple_of(896 * p + 512 * m, 128), 512 - 128 * m)
                bs[i, rows_of(h), lanes] = (dot_nn(g, we[0, :, wide]) + dot_nn(u, we[1, :, wide])).astype(BF16)

                @pl.when(i != ep)
                def _():
                    back_copy(h, i, lanes).start()

                @pl.when(i == ep)
                def _():
                    rb[i, rows_of(h), lanes] = bs[i, rows_of(h), lanes]

    def got_back(h):
        @pl.loop(1, NE)
        def _(k):
            j = (ep + k) % NE

            @pl.when(c == 0)
            def _():
                got(rb.at[j, rows_of(h)], m_r.at[4 + h, j])

            @pl.when(c == 1)
            def _():
                got(rb.at[j, rows_of(h), rest], m_r.at[4 + h, j])

    def h_at(xx, zz):
        return hb.at[(xx * 2 + zz) * 2 + c]

    def send_d(n, xx, zz, dev):
        rc(h_at(xx, zz), h_at(xx, zz), d_s.at[n], d_r.at[n], dev).start()

    def got_d(n, xx, zz):
        got(h_at(xx, zz), d_r.at[n])

    def to_core(n, xx, zz):
        send_d(7 + n, xx, zz, dev_core)

    def d_first():
        for a in range(2):
            k0, k1 = spans[a]
            got(z2r.at[k0:k1], c2_rs.at[a])
        mine = [c0r[x, zh, k].astype(F32) + z2r[k].astype(F32) for k in range(3)]
        hidden, d_gate, d_up = unit_grads(*mine)
        hb[ep, 0] = d_gate
        hb[ep, 1] = d_up
        hb[ep, 2] = hidden
        send_d(0, x, zh, dev_zh)
        send_d(1, x, zh, dev_x(xs))
        send_d(2, x, zh, dev_x(xr))
        to_core(0, x, zh)

    def d_mid():
        got_d(0, x, 1 - zh)
        send_d(3, x, 1 - zh, dev_x(xs))
        send_d(4, x, 1 - zh, dev_x(xr))
        to_core(1, x, 1 - zh)

    def d_forward():
        got_d(1, xr, zh)
        send_d(5, xr, zh, dev_x(xs))
        to_core(2, xr, zh)
        got_d(3, xr, 1 - zh)
        send_d(6, xr, 1 - zh, dev_x(xs))
        to_core(3, xr, 1 - zh)

    def d_end():
        got_d(2, xs, zh)
        to_core(4, xs, zh)
        got_d(4, xs, 1 - zh)
        to_core(5, xs, 1 - zh)
        got_d(5, xo, zh)
        to_core(6, xo, zh)
        got_d(6, xo, 1 - zh)
        to_core(7, xo, 1 - zh)
        sx = (x + 1 + 2 * c) % 4
        sr = (x + 3 + 2 * c) % 4
        for n, (xx, zz) in enumerate(
            ((x, zh), (x, 1 - zh), (sx, zh), (sx, 1 - zh), (sr, zh), (sr, 1 - zh), (xo, zh), (xo, 1 - zh))
        ):
            got(hb.at[(xx * 2 + zz) * 2 + 1 - c], d_r.at[7 + n])

    def input_grads(h):
        @pl.loop(0, 4)
        def _(n):
            g = 8 * h + 2 * n
            back = rb[:, rows_of(h)].reshape(NE * HALF_SLOTS, COVER)
            total = dot_tn(sel[h, :, pl.ds(pl.multiple_of(n * 256, 256), 256)], back)
            for k in range(2):
                both = jnp.concatenate([hb[g, k], hb[g + 1, k]], axis=1)
                total = total + dot_tn(both, wt[k])
            dx[pl.ds(g, 2)] = total.astype(BF16).reshape(2, 4, 2, 16, COVER)

    def e_copy(h, t):
        return rc(dx.at[8 * h : 8 * h + 8, t // 2, t % 2], er.at[h, tp], e_s.at[h, t], e_r.at[h, tp], (ep, t))

    def e_start(h):
        @pl.loop(1, NT)
        def _(k):
            e_copy(h, (tp + k) % NT).start()

    def f_copy(j):
        return rc(fs.at[j], fb.at[ep], f_s.at[j], f_r.at[ep], (j, tp))

    def e_last(h):
        @pl.loop(1, NT)
        def _(k):
            t = (tp + k) % NT
            got(er.at[h, t], e_r.at[h, t])

        half = slice(8 * h, 8 * h + 8)
        er[h, tp] = dx[half, y, zl]
        total = er[h, 0].astype(F32)
        for t in range(1, NT):
            total = total + er[h, t].astype(F32)
        fs[half] = total.astype(BF16)

        @pl.loop(0, 8)
        def _(n):
            j = 8 * h + (ep + n) % 8

            @pl.when(j != ep)
            def _():
                f_copy(j).start()

            @pl.when(j == ep)
            def _():
                fb[j] = fs[j]

    def weight_grads(k):
        gacc[...] = jnp.zeros((FFB, COVER), F32)

        @pl.loop(0, 4)
        def _(n):
            left = jnp.concatenate([hb[4 * n + m, k] for m in range(4)], axis=1)
            rows = xy[0 if k < 2 else 1, pl.ds(4 * n, 4)].reshape(4 * GROUP, COVER)
            gacc[...] += dot_nn(left, rows)

        gdense[k] = (gacc[...] * scale_dense).astype(BF16)

    got_a(0)
    b_zero(0)
    b_first(0, 0)
    b_first(0, 1)
    got_a(1)
    b_zero(1)
    slots()
    b_mid(0, 0)
    b_forward(0, 0, False)
    b_forward(0, 0, True)
    b_mid(0, 1)
    b_first(1, 0)
    b_forward(0, 1, False)
    b_end(0, 0)
    routed(0, 0)
    b_forward(0, 1, True)
    b_mid(1, 0)
    b_first(1, 1)
    b_end(0, 1)
    products(0)
    b_forward(1, 0, False)
    sum_core(0)
    c1_first(0)
    b_forward(1, 0, True)
    routed(0, 1)
    b_mid(1, 1)
    b_forward(1, 1, False)
    c1_second(0)
    b_end(1, 0)
    routed(1, 0)
    b_forward(1, 1, True)
    c1_third(0)
    b_end(1, 1)
    products(1)
    sum_core(1)
    c1_first(1)
    routed(1, 1)
    c1_second(1)
    expert_forward(0)
    c1_third(1)
    expert_back(0)
    d_first()
    expert_forward(1)
    d_mid()
    expert_back(1)

    outs = []
    for a in range(2):
        for p in range(8):
            for m, lanes in enumerate((full, rest)):
                at = 896 * p + 512 * m
                outs.append(
                    pltpu.make_async_copy(
                        mr.at[a, 2 * p + m, :, lanes], erows.at[a, :, at : at + 512 - 128 * m], osem.at[a, 2 * p + m]
                    )
                )
    for o in outs:
        o.start()

    d_forward()
    d_end()
    got_back(0)
    input_grads(0)
    e_start(0)
    weight_grads(0)
    got_back(1)
    input_grads(1)
    e_start(1)
    weight_grads(1)
    e_last(0)
    weight_grads(2)
    e_last(1)

    @pl.loop(1, NE)
    def _(k):
        i = (ep + k) % NE
        got(fb.at[i], f_r.at[i])

    for p in range(8):
        even, odd = fb[2 * p].astype(F32), fb[2 * p + 1].astype(F32)
        at = 896 * p
        gtok[:, at : at + 384] = (cot[:, at : at + 384].astype(F32) + even[:, 0:384]).astype(BF16)
        gtok[:, at + 384 : at + 512] = (
            cot[:, at + 384 : at + 512].astype(F32) + even[:, 384:512] + odd[:, 0:128]
        ).astype(BF16)
        gtok[:, at + 512 : at + 896] = (cot[:, at + 512 : at + 896].astype(F32) + odd[:, 128:512]).astype(BF16)

    for o in outs:
        o.wait()

    @pl.loop(1, NE)
    def _(k):
        j = (ep + k) % NE
        for a in range(2):
            pl.when(j % 2 == 0)(lambda: a_copy(a, k)(full).wait_send())
            pl.when(j % 2 == 1)(lambda: a_copy(a, k)(rest).wait_send())
        sent(route, r_s.at[k])
        f_copy(j).wait_send()
        for h in range(2):
            for a in range(2):

                @pl.when(c == 0)
                def _():
                    m_copy(a, h, j, full).wait_send()

                @pl.when(c == 1)
                def _():
                    m_copy(a, h, j, rest).wait_send()

            @pl.when(j % 2 == 0)
            def _():
                back_copy(h, j, full).wait_send()

            @pl.when(j % 2 == 1)
            def _():
                back_copy(h, j, rest).wait_send()

    for a in range(2):
        for h in range(2):
            for n in range(7):
                sent_b(a, h, n)

            @pl.when(c == 0)
            def _():
                sent(shared(a, h, 384), k_s.at[2 * a + h])

        k0, k1 = spans[a]

        @pl.loop(0, 8)
        def _(p):
            sent(c0r.at[p // 2, p % 2, k0:k1], c0_s.at[a, p])

        for s in c1_sends(a):
            s.wait_send()
        c2_send(a).wait_send()

    @pl.loop(0, 15)
    def _(n):
        sent(h_at(x, zh), d_s.at[n])

    @pl.loop(1, NT)
    def _(k):
        for h in range(2):
            e_copy(h, (tp + k) % NT).wait_send()


def exchange(tokens, cotangent, ids, probs, dgate, dup, ddown, eg, eu, ed, scale_dense):
    vm = lambda shape, dt=BF16: pltpu.VMEM(shape, dt)
    dma = lambda *shape: pltpu.SemaphoreType.DMA(shape)
    width = tokens.shape[1]
    vspec = pl.BlockSpec(memory_space=pltpu.VMEM)
    hspec = pl.BlockSpec(memory_space=pl.ANY)
    return pl.pallas_call(
        functools.partial(kernel, scale_dense),
        name="exchange",
        out_shape=(
            jax.ShapeDtypeStruct(tokens.shape, BF16),
            jax.ShapeDtypeStruct((3, FFB, COVER), BF16),
            jax.ShapeDtypeStruct((3, SLOTS, HID), BF16),
            jax.ShapeDtypeStruct((2, SLOTS, width), BF16),
        ),
        in_specs=[vspec] * 7 + [hspec] * 3,
        out_specs=(vspec, vspec, vspec, hspec),
        scratch_shapes=[
            vm((2, NE, 4, 2, 16, COVER)),
            vm((8, GROUP), F32),
            vm((NE, 8, GROUP), F32),
            vm((3, FFB, COVER)),
            vm((NE, 3, FFB, GROUP)),
            vm((4, 2, 3, FFB, GROUP)),
            vm((2, 3, FFB, GROUP)),
            vm((2, 2, 3, FFB, GROUP)),
            vm((3, FFB, GROUP)),
            vm((NE, 3, FFB, GROUP)),
            vm((2, NE * HALF_SLOTS, 8 * GROUP)),
            vm((2, NE * HALF_SLOTS, 128), F32),
            vm((2, NE, SLOTS, COVER)),
            vm((2, NE, SLOTS, COVER)),
            vm((3, HID, width)),
            vm((3, HALF_SLOTS, HID), F32),
            vm((NE, SLOTS, COVER)),
            vm((NE, SLOTS, COVER)),
            vm((NE, 4, 2, 16, COVER)),
            vm((2, NT, 8, 16, COVER)),
            vm((NE, 16, COVER)),
            vm((NE, 16, COVER)),
            vm((FFB, COVER), F32),
            dma(3),
            dma(2, NE), dma(2, NE),
            dma(NE), dma(NE),
            dma(4, 7), dma(4, 7),
            dma(2, 8), dma(2, 8),
            dma(2, 3), dma(2, 3),
            dma(2), dma(2),
            dma(15), dma(15),
            dma(6, NE), dma(6, NE),
            dma(2, NT), dma(2, NT),
            dma(NE), dma(NE),
            dma(4), dma(4),
            dma(2, NE),
        ],
        compiler_params=pltpu.CompilerParams(
            collective_id=0, has_side_effects=True, vmem_limit_bytes=60 * 1024 * 1024
        ),
    )(tokens, cotangent, ids, probs, dgate, dup, ddown, eg, eu, ed)


def finish_kernel(scale_expert, gtok, gdense, eact, erows, otok, ogate, oup, odown, eg, eu, ed):
    odd = lax.axis_index("ep") % 2

    @pl.when((pl.program_id(0) == 0) & (odd == 0))
    def _():
        for k, o in enumerate((ogate, oup, odown)):
            o[...] = gdense[k, :, 0:448]

    @pl.when((pl.program_id(0) == 0) & (odd == 1))
    def _():
        for k, o in enumerate((ogate, oup, odown)):
            o[...] = gdense[k, :, 64:512]

    otok[...] = gtok[...]
    for k, o in enumerate((eg, eu, ed)):
        o[...] = (dot_tn(eact[k], erows[k // 2]) * scale_expert).astype(BF16)


def finish(gtok, gdense, eact, erows, scale_expert):
    rows, width = gtok.shape
    step = 1024
    whole = lambda *shape: pl.BlockSpec(shape, lambda n: (0,) * len(shape))
    by_step = lambda *shape: pl.BlockSpec(shape + (step,), lambda n: (0,) * len(shape) + (n,))
    return pl.pallas_call(
        functools.partial(finish_kernel, scale_expert),
        name="finish",
        grid=(width // step,),
        in_specs=[by_step(rows), whole(3, FFB, COVER), whole(3, SLOTS, HID), by_step(2, SLOTS)],
        out_specs=[by_step(rows)] + [whole(FFB, 448)] * 3 + [by_step(HID)] * 3,
        out_shape=[jax.ShapeDtypeStruct((rows, width), BF16)]
        + [jax.ShapeDtypeStruct((FFB, 448), BF16)] * 3
        + [jax.ShapeDtypeStruct((HID, width), BF16)] * 3,
        compiler_params=pltpu.CompilerParams(vmem_limit_bytes=60 * 1024 * 1024),
    )(gtok, gdense, eact, erows)


def per_device(
    tokens, cotangent, route_ids, route_probs, dense_gate, dense_up, dense_down, expert_gate, expert_up, expert_down
):
    total_tokens = NE * GROUP
    scale_dense = 1.0 / math.sqrt(total_tokens)
    scale_expert = math.sqrt(NE * NT // 2 / (2.0 * total_tokens))
    gtok, gdense, eact, erows = exchange(
        tokens, cotangent, route_ids.T, route_probs.T, dense_gate.T, dense_up.T, dense_down,
        expert_gate[0], expert_up[0], expert_down[0], scale_dense,
    )
    gtok, ggate, gup, gdown, eg, eu, ed = finish(gtok, gdense, eact, erows, scale_expert)
    return (gtok, ggate.T, gup.T, gdown, eg[None], eu[None], ed[None])


def solution(mesh):
    return jax.shard_map(
        per_device,
        mesh=mesh,
        in_specs=(
            P(("ep", "tp"), None),
            P(("ep", "tp"), None),
            P("ep", None),
            P("ep", None),
            P("ep", "tp"),
            P("ep", "tp"),
            P("tp", "ep"),
            P(("ep", "tp"), None, None),
            P(("ep", "tp"), None, None),
            P(("ep", "tp"), None, None),
        ),
        out_specs=(
            P(("ep", "tp"), None),
            P("ep", "tp"),
            P("ep", "tp"),
            P("tp", "ep"),
            P(("ep", "tp"), None, None),
            P(("ep", "tp"), None, None),
            P(("ep", "tp"), None, None),
        ),
        check_vma=False,
    )
```

time: 216 us -> 174 us (0.81)
  the two profiles are of different devices: /device:TPU:1 before, /device:TPU:119 now
where the time goes in v2:
time: 174 us
  Pallas kernels  173 us (99%)
    pallas_call x1, Pallas kernels, exchange(): pl.pallas_call(functools.partial(kernel, scale_dense), name='exchange', o...  165 us
    pallas_call x1, Pallas kernels, finish(): pl.pallas_call(functools.partial(finish_kernel, scale_expert), name='fini...  8.61 us

profile of v2, /device:TPU:119, one launch (start us, length us, event | category | flops | bytes accessed | tf_op | source)
XLA Modules:
  0.0 173.9 jit_solution(2340848728457258223)
XLA Ops:
  0.6 164.6 %exchange.1 = (bf16[16,7168]{1,0:T(8,128)(2,1)}, bf16[3,304,512]{2,1,0:T(8,128)(2,1)}, bf16[3,96,192]{2,1,0:T(8,128)(2,1)}, bf16[2,96,7168]{2,1,0:T(8,128)(2,1)}) custom-call(bf16[16,7168]{1,0:T(8,128)(2,1)} %tok.1, bf16[16,7168]{1,0:T(8,128)(2,1)} %cot.1, s32[2,128]{1,0:T(2,128)} %bitcast.17, f32[2,128]{1,0:T(2,128)} %bitcast.18, ...), custom_call_target="tpu_custom_call" | custom-call | tf_op jit(solution)/shard_map/exchange/pallas_call | solution.py:673
  165.2 8.6 %finish.1 = (bf16[16,7168]{1,0:T(8,128)(2,1)}, bf16[304,448]{1,0:T(8,128)(2,1)}, bf16[304,448]{1,0:T(8,128)(2,1)}, bf16[304,448]{1,0:T(8,128)(2,1)}, bf16[192,71...) custom-call(bf16[16,7168]{1,0:T(8,128)(2,1)} %get-tuple-element.18.gtok, ...), custom_call_target="tpu_custom_call" | custom-call | tf_op jit(solution)/shard_map/finish/pallas_call | solution.py:751

commit v3 on v2

--- a/solution.py
+++ b/solution.py
@@ -46,7 +46,7 @@
     scale_dense,
     tok, cot, ids, probs, dgate, dup, ddown, eg, eu, ed,
     gtok, gdense, eact, erows,
-    xy, route, rr, wt, part, c0r, x1r, x2r, z2r, hb, sel, sprob, ms, mr, we, eacc, bs, rb, dx, er, fs, fb, gacc,
+    xy, route, rr, wt, wx, gx, part, c0r, x1r, x2r, z2r, hb, sel, sprob, ms, mr, we, eacc, bs, rb, dx, er, fs, fb, gacc,
     wsem, a_s, a_r, r_s, r_r, b_s, b_r, c0_s, c0_rs, c1_s, c1_rs, c2_s, c2_rs, d_s, d_r, m_s, m_r, e_s, e_r, f_s, f_r, k_s, k_r, osem,
 ):
     ep, tp = lax.axis_index("ep"), lax.axis_index("tp")
@@ -95,6 +95,7 @@
     @pl.when(c == 1)
     def _():
         rb[:, :, 0:128] = jnp.zeros((NE, SLOTS, 128), BF16)
+        xy[:, :, :, :, :, 0:128] = jnp.zeros((2, NE, 4, 2, 16, 128), BF16)
 
     barrier = pltpu.get_barrier_semaphore()
 
@@ -154,6 +155,16 @@
         rc(route, rr.at[ep], r_s.at[k], r_r.at[k], ((ep + k) % NE, tp)).start()
 
     a_send(1)
+    def w_copy():
+        return rc(wt.at[:, :, 0:128], wx, k_s.at[0], k_r.at[0], dev_core)
+
+    def w_join():
+        @pl.when(c == 0)
+        def _():
+            got(wx, k_r.at[0])
+            for k in range(3):
+                wt[k, :, 384:512] = wt[k, :, 384:512] + wx[k]
+
     blank = jnp.zeros((FFB, COVER - 448), BF16)
 
     @pl.when(c == 0)
@@ -165,6 +176,7 @@
     def _():
         for k, w in enumerate((dgate, dup, ddown)):
             wt[k] = jnp.concatenate([blank, w[...]], axis=1)
+        w_copy().start()
 
     rr[ep] = route[...]
 
@@ -209,21 +221,10 @@
             send_b(a, h, 5, yr, zl, dev_y(ys))
             got_b(a, h, 2, ys, zl)
 
-    def shared(a, h, at):
-        return xy.at[a, 8 * h : 8 * h + 8, :, :, :, at : at + 128]
-
     def b_end(a, h):
         got_b(a, h, 5, yo, zl)
         got_b(a, h, 4, ys, 1 - zl)
         got_b(a, h, 6, yo, 1 - zl)
-
-        @pl.when(c == 0)
-        def _():
-            rc(shared(a, h, 384), shared(a, h, 0), k_s.at[2 * a + h], k_r.at[2 * a + h], dev_core).start()
-
-        @pl.when(c == 1)
-        def _():
-            got(shared(a, h, 0), k_r.at[2 * a + h])
 
     def slots():
         @pl.loop(1, NE)
@@ -252,11 +253,14 @@
 
         @pl.loop(0, 8)
         def _(p):
-            rows = xy[a, pl.ds(2 * p, 2)].reshape(2 * GROUP, COVER)
-            for k in range(k0, k1):
-                res = dot_nt(wt[k], rows).astype(BF16)
-                part[2 * p, k] = res[:, :GROUP]
-                part[2 * p + 1, k] = res[:, GROUP:]
+            def act(lanes):
+                rows = xy[a, pl.ds(2 * p, 2), :, :, :, lanes].reshape(2 * GROUP, lanes.stop - lanes.start)
+                for k in range(k0, k1):
+                    res = dot_nt(wt[k, :, lanes], rows).astype(BF16)
+                    part[2 * p, k] = res[:, :GROUP]
+                    part[2 * p + 1, k] = res[:, GROUP:]
+
+            by_core(act)
             rc(
                 part.at[2 * p + 1 - c, k0:k1], c0r.at[p // 2, p % 2, k0:k1], c0_s.at[a, p], c0_rs.at[a, p], dev_core
             ).start()
@@ -444,68 +448,74 @@
         send_d(6, xr, 1 - zh, dev_x(xs))
         to_core(3, xr, 1 - zh)
 
-    def d_end():
+    def d_sides():
         got_d(2, xs, zh)
         to_core(4, xs, zh)
         got_d(4, xs, 1 - zh)
         to_core(5, xs, 1 - zh)
+
+    def d_far():
         got_d(5, xo, zh)
         to_core(6, xo, zh)
         got_d(6, xo, 1 - zh)
         to_core(7, xo, 1 - zh)
-        sx = (x + 1 + 2 * c) % 4
-        sr = (x + 3 + 2 * c) % 4
-        for n, (xx, zz) in enumerate(
-            ((x, zh), (x, 1 - zh), (sx, zh), (sx, 1 - zh), (sr, zh), (sr, 1 - zh), (xo, zh), (xo, 1 - zh))
-        ):
-            got(hb.at[(xx * 2 + zz) * 2 + 1 - c], d_r.at[7 + n])
-
-    def input_grads(h):
-        @pl.loop(0, 4)
+
+    def d_core(n, xx):
+        got(hb.at[(xx * 2 + zh) * 2 + 1 - c], d_r.at[7 + n])
+        got(hb.at[(xx * 2 + 1 - zh) * 2 + 1 - c], d_r.at[8 + n])
+
+    def input_grads(xx):
+        h = xx // 2
+
+        @pl.loop(0, 2)
         def _(n):
-            g = 8 * h + 2 * n
-            back = rb[:, rows_of(h)].reshape(NE * HALF_SLOTS, COVER)
-            total = dot_tn(sel[h, :, pl.ds(pl.multiple_of(n * 256, 256), 256)], back)
+            g = 4 * xx + 2 * n
+            back = rb[:, pl.ds(pl.multiple_of(HALF_SLOTS * h, 16), HALF_SLOTS)].reshape(NE * HALF_SLOTS, COVER)
+            at = pl.multiple_of((xx % 2) * 512 + n * 256, 256)
+            total = dot_tn(sel[h, :, pl.ds(at, 256)], back)
             for k in range(2):
                 both = jnp.concatenate([hb[g, k], hb[g + 1, k]], axis=1)
                 total = total + dot_tn(both, wt[k])
             dx[pl.ds(g, 2)] = total.astype(BF16).reshape(2, 4, 2, 16, COVER)
 
-    def e_copy(h, t):
-        return rc(dx.at[8 * h : 8 * h + 8, t // 2, t % 2], er.at[h, tp], e_s.at[h, t], e_r.at[h, tp], (ep, t))
-
-    def e_start(h):
+    def e_copy(xx, t, lanes):
+        src = dx.at[pl.ds(4 * xx, 4), t // 2, t % 2, :, lanes]
+        return rc(src, er.at[xx, tp, :, :, lanes], e_s.at[xx, t], e_r.at[xx, tp], (ep, t))
+
+    def e_start(xx):
         @pl.loop(1, NT)
         def _(k):
-            e_copy(h, (tp + k) % NT).start()
-
-    def f_copy(j):
-        return rc(fs.at[j], fb.at[ep], f_s.at[j], f_r.at[ep], (j, tp))
-
-    def e_last(h):
+            by_core(lambda lanes: e_copy(xx, (tp + k) % NT, lanes).start())
+
+    def f_copy(j, lanes):
+        return rc(fs.at[j, :, lanes], fb.at[ep, :, lanes], f_s.at[j], f_r.at[ep], (j, tp))
+
+    def e_last(xx):
         @pl.loop(1, NT)
         def _(k):
             t = (tp + k) % NT
-            got(er.at[h, t], e_r.at[h, t])
-
-        half = slice(8 * h, 8 * h + 8)
-        er[h, tp] = dx[half, y, zl]
-        total = er[h, 0].astype(F32)
+            by_core(lambda lanes: got(er.at[xx, t, :, :, lanes], e_r.at[xx, t]))
+
+        er[xx, tp] = dx[pl.ds(4 * xx, 4), y, zl]
+        total = er[xx, 0].astype(F32)
         for t in range(1, NT):
-            total = total + er[h, t].astype(F32)
-        fs[half] = total.astype(BF16)
-
-        @pl.loop(0, 8)
+            total = total + er[xx, t].astype(F32)
+        fs[pl.ds(4 * xx, 4)] = total.astype(BF16)
+
+        @pl.loop(0, 4)
         def _(n):
-            j = 8 * h + (ep + n) % 8
+            j = 4 * xx + (ep + n) % 4
 
             @pl.when(j != ep)
             def _():
-                f_copy(j).start()
+                by_core(lambda lanes: f_copy(j, lanes).start())
 
             @pl.when(j == ep)
             def _():
                 fb[j] = fs[j]
+
+    def g_copy():
+        return rc(gdense.at[:, :, 384:512], gx, k_s.at[1], k_r.at[1], dev_core)
 
     def weight_grads(k):
         gacc[...] = jnp.zeros((FFB, COVER), F32)
@@ -517,6 +527,8 @@
             gacc[...] += dot_nn(left, rows)
 
         gdense[k] = (gacc[...] * scale_dense).astype(BF16)
+        if k == 2:
+            pl.when(c == 0)(lambda: g_copy().start())
 
     got_a(0)
     b_zero(0)
@@ -537,6 +549,7 @@
     b_mid(1, 0)
     b_first(1, 1)
     b_end(0, 1)
+    w_join()
     products(0)
     b_forward(1, 0, False)
     sum_core(0)
@@ -551,18 +564,19 @@
     b_forward(1, 1, True)
     c1_third(0)
     b_end(1, 1)
+    routed(1, 1)
     products(1)
     sum_core(1)
     c1_first(1)
-    routed(1, 1)
+    expert_forward(0)
     c1_second(1)
-    expert_forward(0)
+    expert_back(0)
     c1_third(1)
-    expert_back(0)
     d_first()
     expert_forward(1)
+    expert_back(1)
     d_mid()
-    expert_back(1)
+    d_forward()
 
     outs = []
     for a in range(2):
@@ -577,33 +591,45 @@
     for o in outs:
         o.start()
 
-    d_forward()
-    d_end()
+    d_sides()
+    d_core(0, x)
     got_back(0)
-    input_grads(0)
-    e_start(0)
+    got_back(1)
+    input_grads(x)
+    e_start(x)
+    d_core(2, xs)
+    d_core(4, xr)
+    input_grads(xr)
+    e_start(xr)
+    d_far()
+    input_grads(xs)
+    e_start(xs)
+    d_core(6, xo)
+    input_grads(xo)
+    e_start(xo)
     weight_grads(0)
-    got_back(1)
-    input_grads(1)
-    e_start(1)
+    e_last(x)
     weight_grads(1)
-    e_last(0)
+    e_last(xr)
     weight_grads(2)
-    e_last(1)
+    e_last(xs)
+    e_last(xo)
 
     @pl.loop(1, NE)
     def _(k):
         i = (ep + k) % NE
-        got(fb.at[i], f_r.at[i])
+        pl.when(i % 2 == 0)(lambda: got(fb.at[i], f_r.at[i]))
+        pl.when(i % 2 == 1)(lambda: got(fb.at[i, :, rest], f_r.at[i]))
 
     for p in range(8):
-        even, odd = fb[2 * p].astype(F32), fb[2 * p + 1].astype(F32)
-        at = 896 * p
-        gtok[:, at : at + 384] = (cot[:, at : at + 384].astype(F32) + even[:, 0:384]).astype(BF16)
-        gtok[:, at + 384 : at + 512] = (
-            cot[:, at + 384 : at + 512].astype(F32) + even[:, 384:512] + odd[:, 0:128]
-        ).astype(BF16)
-        gtok[:, at + 512 : at + 896] = (cot[:, at + 512 : at + 896].astype(F32) + odd[:, 128:512]).astype(BF16)
+        for m, lanes in enumerate((full, rest)):
+            at = slice(896 * p + 512 * m, 896 * p + 512 + 384 * m)
+            gtok[:, at] = (cot[:, at].astype(F32) + fb[2 * p + m, :, lanes].astype(F32)).astype(BF16)
+
+    @pl.when(c == 1)
+    def _():
+        got(gx, k_r.at[1])
+        gdense[:, :, 0:128] = gx[...]
 
     for o in outs:
         o.wait()
@@ -615,7 +641,7 @@
             pl.when(j % 2 == 0)(lambda: a_copy(a, k)(full).wait_send())
             pl.when(j % 2 == 1)(lambda: a_copy(a, k)(rest).wait_send())
         sent(route, r_s.at[k])
-        f_copy(j).wait_send()
+        by_core(lambda lanes: f_copy(j, lanes).wait_send())
         for h in range(2):
             for a in range(2):
 
@@ -640,10 +666,6 @@
             for n in range(7):
                 sent_b(a, h, n)
 
-            @pl.when(c == 0)
-            def _():
-                sent(shared(a, h, 384), k_s.at[2 * a + h])
-
         k0, k1 = spans[a]
 
         @pl.loop(0, 8)
@@ -660,8 +682,16 @@
 
     @pl.loop(1, NT)
     def _(k):
-        for h in range(2):
-            e_copy(h, (tp + k) % NT).wait_send()
+        for n in range(4):
+            by_core(lambda lanes: e_copy(n, (tp + k) % NT, lanes).wait_send())
+
+    @pl.when(c == 0)
+    def _():
+        g_copy().wait_send()
+
+    @pl.when(c == 1)
+    def _():
+        w_copy().wait_send()
 
 
 def exchange(tokens, cotangent, ids, probs, dgate, dup, ddown, eg, eu, ed, scale_dense):
@@ -686,6 +716,8 @@
             vm((8, GROUP), F32),
             vm((NE, 8, GROUP), F32),
             vm((3, FFB, COVER)),
+            vm((3, FFB, 128)),
+            vm((3, FFB, 128)),
             vm((NE, 3, FFB, GROUP)),
             vm((4, 2, 3, FFB, GROUP)),
             vm((2, 3, FFB, GROUP)),
@@ -701,7 +733,7 @@
             vm((NE, SLOTS, COVER)),
             vm((NE, SLOTS, COVER)),
             vm((NE, 4, 2, 16, COVER)),
-            vm((2, NT, 8, 16, COVER)),
+            vm((4, NT, 4, 16, COVER)),
             vm((NE, 16, COVER)),
             vm((NE, 16, COVER)),
             vm((FFB, COVER), F32),
@@ -714,9 +746,9 @@
             dma(2), dma(2),
             dma(15), dma(15),
             dma(6, NE), dma(6, NE),
-            dma(2, NT), dma(2, NT),
+            dma(4, NT), dma(4, NT),
             dma(NE), dma(NE),
-            dma(4), dma(4),
+            dma(2), dma(2),
             dma(2, NE),
         ],
         compiler_params=pltpu.CompilerParams(

time: 174 us -> 162 us (0.931)
  the two profiles are of different devices: /device:TPU:119 before, /device:TPU:1 now
where the time goes in v3:
time: 162 us
  Pallas kernels  161 us (99%)
    pallas_call x1, Pallas kernels, exchange(): pl.pallas_call(functools.partial(kernel, scale_dense), name='exchange', o...  152 us
    pallas_call x1, Pallas kernels, finish(): pl.pallas_call(functools.partial(finish_kernel, scale_expert), name='fini...  8.6 us

profile of v3, /device:TPU:1, one launch (start us, length us, event | category | flops | bytes accessed | tf_op | source)
XLA Modules:
  0.0 161.7 jit_solution(8315993812840259137)
XLA Ops:
  0.6 152.5 %exchange.1 = (bf16[16,7168]{1,0:T(8,128)(2,1)}, bf16[3,304,512]{2,1,0:T(8,128)(2,1)}, bf16[3,96,192]{2,1,0:T(8,128)(2,1)}, bf16[2,96,7168]{2,1,0:T(8,128)(2,1)}) custom-call(bf16[16,7168]{1,0:T(8,128)(2,1)} %tok.1, bf16[16,7168]{1,0:T(8,128)(2,1)} %cot.1, s32[2,128]{1,0:T(2,128)} %bitcast.17, f32[2,128]{1,0:T(2,128)} %bitcast.18, ...), custom_call_target="tpu_custom_call" | custom-call | tf_op jit(solution)/shard_map/exchange/pallas_call | solution.py:703
  153.1 8.6 %finish.1 = (bf16[16,7168]{1,0:T(8,128)(2,1)}, bf16[304,448]{1,0:T(8,128)(2,1)}, bf16[304,448]{1,0:T(8,128)(2,1)}, bf16[304,448]{1,0:T(8,128)(2,1)}, bf16[192,71...) custom-call(bf16[16,7168]{1,0:T(8,128)(2,1)} %get-tuple-element.18.gtok, ...), custom_call_target="tpu_custom_call" | custom-call | tf_op jit(solution)/shard_map/finish/pallas_call | solution.py:783

commit v4 on v3

--- a/solution.py
+++ b/solution.py
@@ -562,10 +562,10 @@
     b_end(1, 0)
     routed(1, 0)
     b_forward(1, 1, True)
-    c1_third(0)
     b_end(1, 1)
     routed(1, 1)
     products(1)
+    c1_third(0)
     sum_core(1)
     c1_first(1)
     expert_forward(0)
@@ -777,7 +777,7 @@
 
 def finish(gtok, gdense, eact, erows, scale_expert):
     rows, width = gtok.shape
-    step = 1024
+    step = 3584
     whole = lambda *shape: pl.BlockSpec(shape, lambda n: (0,) * len(shape))
     by_step = lambda *shape: pl.BlockSpec(shape + (step,), lambda n: (0,) * len(shape) + (n,))
     return pl.pallas_call(

time: 162 us -> 158 us (0.975)
  Pallas kernels: 161 us -> 157 us
    pallas_call x1, Pallas kernels: 8.6 us -> 6.41 us  [finish(): pl.pallas_call(functools.partial(finish_kernel, scale_expert), name='fini...]
    pallas_call x1, Pallas kernels: 152 us -> 151 us  [exchange(): pl.pallas_call(functools.partial(kernel, scale_dense), name='exchange', o...]
where the time goes in v4:
time: 158 us
  Pallas kernels  157 us (99%)
    pallas_call x1, Pallas kernels, exchange(): pl.pallas_call(functools.partial(kernel, scale_dense), name='exchange', o...  151 us
    pallas_call x1, Pallas kernels, finish(): pl.pallas_call(functools.partial(finish_kernel, scale_expert), name='fini...  6.41 us

profile of v4, /device:TPU:1, one launch (start us, length us, event | category | flops | bytes accessed | tf_op | source)
XLA Modules:
  0.0 157.9 jit_solution(10239500344051426731)
XLA Ops:
  0.6 150.8 %exchange.1 = (bf16[16,7168]{1,0:T(8,128)(2,1)}, bf16[3,304,512]{2,1,0:T(8,128)(2,1)}, bf16[3,96,192]{2,1,0:T(8,128)(2,1)}, bf16[2,96,7168]{2,1,0:T(8,128)(2,1)}) custom-call(bf16[16,7168]{1,0:T(8,128)(2,1)} %tok.1, bf16[16,7168]{1,0:T(8,128)(2,1)} %cot.1, s32[2,128]{1,0:T(2,128)} %bitcast.17, f32[2,128]{1,0:T(2,128)} %bitcast.18, ...), custom_call_target="tpu_custom_call" | custom-call | tf_op jit(solution)/shard_map/exchange/pallas_call | solution.py:703
  151.4 6.4 %finish.1 = (bf16[16,7168]{1,0:T(8,128)(2,1)}, bf16[304,448]{1,0:T(8,128)(2,1)}, bf16[304,448]{1,0:T(8,128)(2,1)}, bf16[304,448]{1,0:T(8,128)(2,1)}, bf16[192,71...) custom-call(bf16[16,7168]{1,0:T(8,128)(2,1)} %get-tuple-element.18.gtok, ...), custom_call_target="tpu_custom_call" | custom-call | tf_op jit(solution)/shard_map/finish/pallas_call | solution.py:783

commit v5 on v4

--- a/solution.py
+++ b/solution.py
@@ -92,21 +92,21 @@
     for w in loads:
         w.start()
 
+    barrier = pltpu.get_barrier_semaphore()
+
+    @pl.loop(1, NE)
+    def _(k):
+        pl.semaphore_signal(barrier, inc=1, device_id=((ep + k) % NE, tp), device_id_type=MESH)
+
+    @pl.loop(1, NT)
+    def _(k):
+        pl.semaphore_signal(barrier, inc=1, device_id=(ep, (tp + k) % NT), device_id_type=MESH)
+
+
     @pl.when(c == 1)
     def _():
         rb[:, :, 0:128] = jnp.zeros((NE, SLOTS, 128), BF16)
         xy[:, :, :, :, :, 0:128] = jnp.zeros((2, NE, 4, 2, 16, 128), BF16)
-
-    barrier = pltpu.get_barrier_semaphore()
-
-    @pl.loop(1, NE)
-    def _(k):
-        pl.semaphore_signal(barrier, inc=1, device_id=((ep + k) % NE, tp), device_id_type=MESH)
-
-    @pl.loop(1, NT)
-    def _(k):
-        pl.semaphore_signal(barrier, inc=1, device_id=(ep, (tp + k) % NT), device_id_type=MESH)
-
 
     pl.semaphore_wait(barrier, NE - 1 + NT - 1)
 
@@ -599,9 +599,9 @@
     e_start(x)
     d_core(2, xs)
     d_core(4, xr)
+    d_far()
     input_grads(xr)
     e_start(xr)
-    d_far()
     input_grads(xs)
     e_start(xs)
     d_core(6, xo)

time: 158 us -> 158 us (level)
  no operation moved by 1% of the time
where the time goes in v5:
time: 158 us; the launch traced here: 157 us
  Pallas kernels  157 us (99%)
    pallas_call x1, Pallas kernels, exchange(): pl.pallas_call(functools.partial(kernel, scale_dense), name='exchange', o...  150 us
    pallas_call x1, Pallas kernels, finish(): pl.pallas_call(functools.partial(finish_kernel, scale_expert), name='fini...  6.41 us

profile of v5, /device:TPU:1, one launch (start us, length us, event | category | flops | bytes accessed | tf_op | source)
XLA Modules:
  0.0 157.4 jit_solution(7035010075508269602)
XLA Ops:
  0.6 150.4 %exchange.1 = (bf16[16,7168]{1,0:T(8,128)(2,1)}, bf16[3,304,512]{2,1,0:T(8,128)(2,1)}, bf16[3,96,192]{2,1,0:T(8,128)(2,1)}, bf16[2,96,7168]{2,1,0:T(8,128)(2,1)}) custom-call(bf16[16,7168]{1,0:T(8,128)(2,1)} %tok.1, bf16[16,7168]{1,0:T(8,128)(2,1)} %cot.1, s32[2,128]{1,0:T(2,128)} %bitcast.17, f32[2,128]{1,0:T(2,128)} %bitcast.18, ...), custom_call_target="tpu_custom_call" | custom-call | tf_op jit(solution)/shard_map/exchange/pallas_call | solution.py:703
  151.0 6.4 %finish.1 = (bf16[16,7168]{1,0:T(8,128)(2,1)}, bf16[304,448]{1,0:T(8,128)(2,1)}, bf16[304,448]{1,0:T(8,128)(2,1)}, bf16[304,448]{1,0:T(8,128)(2,1)}, bf16[192,71...) custom-call(bf16[16,7168]{1,0:T(8,128)(2,1)} %get-tuple-element.18.gtok, ...), custom_call_target="tpu_custom_call" | custom-call | tf_op jit(solution)/shard_map/finish/pallas_call | solution.py:783
